TPU v7x, 32 devices: a whole 2x2x4 slice. The times are simulated.
32 devices in a mesh: ctx: 4 (over z), ch: 8 (over y, x, core).
Axes of the slice: x: 2, y: 2, z: 4, core: 2. Of those that a mesh axis runs over, the one named last changes fastest.
Arguments:
- features: bfloat16 [2, 4, 128, 3, 4096], P(None, 'ctx', None, None, 'ch'), may hold values from -6 to 6
- short_weight: bfloat16 [7, 3, 4096], P(None, None, 'ch'), may hold values from -2 to 2
- long_filter: bfloat16 [2, 4, 128, 4096], P(None, 'ctx', None, 'ch'), may hold values from -0.25 to 0.25
- skip_gain: float32 [4096], P('ch'), may hold values from -4 to 4
- out_weight: bfloat16 [4096, 4096], P('ch'), may hold values from -0.125 to 0.125
Outputs:
- mixed: bfloat16 [2, 4, 128, 4096], P(None, 'ctx', None, 'ch')
All inputs are finite; a program needn't handle non-finite values.
Results may differ from a plain program's by a relative error of at most 0.015.
Values may be sent and summed in bfloat16 or wider, within the bound.
A program may use at most 128 MiB of HBM per device.

v0:
```python
import math

import jax
import jax.numpy as jnp
from jax import lax
from jax.sharding import PartitionSpec as P


def from_behind(value, axis, steps):
    count = lax.axis_size(axis)
    initial, last = (max(0, -steps), min(count, count - steps))
    return lax.ppermute(value, axis, [(source, source + steps) for source in range(initial, last)])


def transform_tables(length):
    period = 2 * length
    indices = jnp.arange(period, dtype=jnp.int32)
    phases = indices[:, None] * indices[None, :] % period
    angles = phases.astype(jnp.float32) * (2.0 * math.pi / period)
    cosine = jnp.cos(angles)
    sine_table = jnp.sin(angles)
    forward_full = jnp.concatenate([cosine, -sine_table], axis=0)
    forward_data = forward_full[:, :length]
    inverse = jnp.concatenate([cosine[:length], -sine_table[:length]], axis=1) / period
    return (forward_full, forward_data, inverse)


def complex_product(first, second):
    middle = first.shape[-2] // 2
    real_a = first[..., :middle, :]
    imag_a = first[..., middle:, :]
    real_b = second[..., :middle, :]
    imag_b = second[..., middle:, :]
    return jnp.concatenate(
        [real_a * real_b - imag_a * imag_b, real_a * imag_b + imag_a * real_b], axis=-2
    )


def featurize(tokens, before, kernel):
    extended = jnp.concatenate([before, tokens], axis=0).astype(jnp.float32)
    length = tokens.shape[0]
    margin_rows = kernel.shape[0] - 1
    summed = jnp.zeros(tokens.shape, jnp.float32)
    for offset in range(kernel.shape[0]):
        summed = (
            summed
            + kernel[offset].astype(jnp.float32)
            * extended[margin_rows - offset : margin_rows - offset + length]
        )
    return summed


def ordered(blocks):
    return jnp.concatenate([blocks[0], jnp.flip(blocks[1], axis=0)], axis=0)


def local(features, short_weight, long_filter, skip_gain, out_weight):
    pair_count = lax.axis_size("ctx")
    blocks_all = 2 * pair_count
    position = lax.axis_index("ctx")
    length = features.shape[2]
    margin_rows = short_weight.shape[0] - 1
    trailing = features[:, 0, length - margin_rows :]
    from_before = from_behind(trailing[0], "ctx", 1)
    from_after = from_behind(trailing[1], "ctx", -1)
    second_rim = jnp.where(position == pair_count - 1, trailing[0], from_after)
    first_feat = featurize(features[0, 0], from_before, short_weight)
    second_feat = featurize(features[1, 0], second_rim, short_weight)
    featured = jnp.stack([first_feat, second_feat], axis=0)
    queries = featured[:, :, 0]
    gated_keys = (featured[:, :, 1] * featured[:, :, 2]).astype(jnp.bfloat16)
    forward_full, forward_data, inverse = transform_tables(length)
    precise = lax.Precision.HIGHEST
    moved_gated, moved_filter = (
        lax.all_to_all(gated_keys[:, None], "ctx", split_axis=3, concat_axis=1, tiled=True),
        lax.all_to_all(long_filter, "ctx", split_axis=3, concat_axis=1, tiled=True),
    )
    ordered_gated = ordered(moved_gated).astype(jnp.float32)
    lag_order = ordered(moved_filter)
    padded = jnp.concatenate(
        [jnp.zeros((1,) + lag_order.shape[1:], lag_order.dtype), lag_order], axis=0
    )
    segments = jnp.concatenate([padded[1:], padded[:-1]], axis=1).astype(jnp.float32)
    responses = jnp.einsum("fm,kmc->kfc", forward_full, segments, precision=precise)
    spectra = jnp.einsum("fn,knc->kfc", forward_data, ordered_gated, precision=precise)
    sources = jnp.arange(blocks_all, dtype=jnp.int32)

    def one_target(target):
        distance = target - sources
        picked = jnp.take(responses, jnp.maximum(distance, 0), axis=0)
        products = complex_product(picked, spectra)
        summed = jnp.sum(jnp.where((distance >= 0)[:, None, None], products, 0.0), axis=0)
        return jnp.dot(inverse, summed, precision=precise)

    group_size = math.gcd(blocks_all, 8)
    grouped = sources.reshape(blocks_all // group_size, group_size)
    outputs = lax.map(jax.vmap(one_target), grouped).reshape(
        (blocks_all, length, responses.shape[-1])
    )
    blocks = jnp.stack([outputs[:pair_count], jnp.flip(outputs[pair_count:], axis=0)], axis=0)
    returned = lax.all_to_all(blocks, "ctx", split_axis=1, concat_axis=3, tiled=True)
    convolved = returned[:, 0]
    activated = (queries * (convolved + skip_gain * gated_keys.astype(jnp.float32))).astype(
        jnp.bfloat16
    )
    token_rows = activated.reshape(2 * length, activated.shape[-1])
    channels = token_rows.shape[1]
    owned = lax.psum_scatter(
        lax.dot_general(
            out_weight, token_rows, (((0,), (1,)), ((), ())), preferred_element_type=jnp.float32
        ).astype(jnp.bfloat16),
        "ch",
        scatter_dimension=0,
        tiled=True,
    ).astype(jnp.float32)
    result = owned.T
    return result.astype(jnp.bfloat16).reshape(2, 1, length, channels)


def solution(mesh):
    in_specs = (
        P(None, "ctx", None, None, "ch"),
        P(None, None, "ch"),
        P(None, "ctx", None, "ch"),
        P("ch"),
        P("ch", None),
    )
    out_specs = P(None, "ctx", None, "ch")
    return jax.shard_map(local, mesh=mesh, in_specs=in_specs, out_specs=out_specs, check_vma=False)
```

profile of v0, /device:TPU:0, one launch (start us, length us, event | category | flops | bytes accessed | tf_op | source)
XLA Modules:
  0.0 151.7 jit_solution(16035138713991080439)
XLA Ops:
  6.5 1.8 %copy.33 = bf16[2,1,128,512]{2,0,1,3:T(2,128)(2,1)} copy(bf16[2,1,128,512]{3,2,1,0:T(8,128)(2,1)} %param.7) | data formatting | bytes 524288 | tf_op args[2]
  8.4 6.3 %all-to-all-start = ((bf16[2,1,128,512]{2,0,1,3:T(2,128)(2,1)}), bf16[2,1,128,512]{2,0,1,3:T(2,128)(2,1)S(1)}, u32[]{:S(2)}, u32[]{:S(2)}) async-start(bf16[2,1,128,512]{2,0,1,3:T(2,128)(2,1)} %copy.33), calls=%async_computation | async-start | bytes 524288 | tf_op jit(solution)/shard_map/all_to_all | solution.py:76
  14.7 0.8 fusion.56
  15.7 4.0 %collective-permute-start = (bf16[6,3,512]{0,2,1:T(8,128)(2,1)S(1)}, bf16[6,3,512]{0,2,1:T(8,128)(2,1)S(1)}, u32[]{:S(2)}, u32[]{:S(2)}) collective-permute-start(bf16[6,3,512]{0,2,1:T(8,128)(2,1)S(1)} %bitcast.98), channel_id=1, source_target_pairs={{0,8},{8,16},{16,24},{1,9},{9,17},{17,25},{2,10},{10,18},{18,26},{... | collective-permute-start | bytes 55304 | tf_op jit(solution)/shard_map/ppermute | solution.py:12
  19.9 1.3 collective-permute-start.1
  21.2 1.0 fusion.45
  22.3 1.2 fusion.55
  23.5 1.0 fusion.44
  24.6 0.7 slice_negate_fusion
  25.8 0.7 slice.208
  26.4 5.7 %collective-permute-done.1 = bf16[6,3,512]{0,2,1:T(8,128)(2,1)} collective-permute-done((bf16[6,3,512]{0,2,1:T(8,128)(2,1)S(1)}, bf16[6,3,512]{0,2,1:T(8,128)(2,1)}, u32[]{:S(2)}, u32[]{:S(2)}) %collective-permute-start.1) | collective-permute-done | bytes 18464 | tf_op jit(solution)/shard_map/ppermute | solution.py:12
  32.1 1.0 broadcast_select_fusion.1
  33.5 0.3 maximum_convert_fusion
  33.8 3.0 %fusion.8 = f32[128,3,512]{0,2,1:T(8,128)S(1)} fusion(f32[134,3,512]{0,2,1:T(8,128)S(1)} %maximum_convert_fusion, f32[3,512]{1,0:T(4,128)S(1)} %get-tuple-element.51, f32[3,512]{1,0:T(4,128)S(1)} %get-tuple-element.52, f32[3,512]{1,0:T(4,128)S(1)} %get-tuple-element.53, f32[3,512]{1,0:T(4,128)S(1)} %get-tuple-element.54, f32[3,512]{1,0:T(4,128)S(1)} %get-tuple-element.55, ...), kind=kLoop, calls=%fused_computation.29 | loop fusion | flops 2555904 | bytes 6334464 | tf_op jit(solution)/shard_map/add | solution.py:46
  36.8 3.0 %fusion.2 = f32[128,3,512]{0,2,1:T(8,128)S(1)} fusion(f32[134,3,512]{0,2,1:T(8,128)S(1)} %maximum_convert_fusion.1, f32[3,512]{1,0:T(4,128)S(1)} %get-tuple-element.51, f32[3,512]{1,0:T(4,128)S(1)} %get-tuple-element.52, f32[3,512]{1,0:T(4,128)S(1)} %get-tuple-element.53, f32[3,512]{1,0:T(4,128)S(1)} %get-tuple-element.54, ...), kind=kLoop, calls=%fused_computation.16 | loop fusion | flops 2555904 | bytes 6334464 | tf_op jit(solution)/shard_map/add | solution.py:46
  39.8 2.1 %fusion.18 = (f32[2,128,1,512]{1,0,3,2:T(2,128)S(1)}, bf16[2,128,1,512]{1,0,3,2:T(2,128)(2,1)}) fusion(f32[1,128,3,512]{1,0,3,2:T(1,128)S(1)} %bitcast.92, f32[1,128,3,512]{1,0,3,2:T(1,128)S(1)} %bitcast.93), kind=kLoop, calls=%fused_computation.49 | loop fusion | flops 655360 | bytes 2359296 | tf_op jit(solution)/shard_map/stack | solution.py:69
  41.8 4.2 %all-to-all-start.1 = ((bf16[2,1,128,512]{2,0,1,3:T(2,128)(2,1)}), bf16[2,1,128,512]{2,0,1,3:T(2,128)(2,1)}, u32[]{:S(2)}, u32[]{:S(2)}) async-start(bf16[2,1,128,512]{2,0,1,3:T(2,128)(2,1)} %bitcast.17), calls=%async_computation.1 | async-start | bytes 524288 | tf_op jit(solution)/shard_map/all_to_all | solution.py:75
  46.3 1.1 convolution_bitcast_fusion
  47.3 7.4 %gather_fusion = f32[64,512,128]{1,2,0:T(8,128)} fusion(f32[8,512,128]{1,2,0:T(8,128)S(1)} %convolution_bitcast_fusion, s32[1024]{0:T(1024)S(1)} %pad_clamp_fusion), kind=kCustom, calls=%fused_computation | custom fusion | bytes 33554688 | tf_op jit(solution)/shard_map/while/body/eval_jaxpr/vmap(jit(_take))/gather | solution.py:90
  54.7 12.1 %broadcast_select_fusion = f32[8,8,512,128]{2,3,1,0:T(8,128)} fusion(f32[8,8,512,128]{2,3,1,0:T(8,128)} %bitcast.91, pred[8,8]{1,0:T(8,128)(4,1)S(1)} %maximum_compare_fusion), kind=kLoop, calls=%fused_computation.5 | loop fusion | flops 4194304 | bytes 33554496 | tf_op jit(solution)/shard_map/while/body/eval_jaxpr/vmap(jit(_take))/select_n | solution.py:90
  66.8 1.0 copy.35
  67.8 1.0 convolution_bitcast_fusion.1
  69.0 7.4 %multiply_subtract_fusion = (f32[8,8,256,128]{2,3,1,0:T(8,128)S(1)}, f32[8,8,256,128]{2,3,1,0:T(8,128)S(1)}) fusion(f32[8,8,512,128]{2,3,1,0:T(8,128)} %broadcast_select_fusion, f32[8,256,128]{1,2,0:T(8,128)S(1)} %get-tuple-element.20, f32[8,256,128]{1,2,0:T(8,128)S(1)} %get-tuple-element.19), kind=kLoop, calls=%fused_computation.4 | loop fusion | flops 12582912 | bytes 35651584 | tf_op jit(solution)/shard_map/while/body/eval_jaxpr/vmap()/sub | solution.py:35
  76.5 1.8 %fusion = f32[8,512,128]{1,2,0:T(8,128)S(1)} fusion(f32[8,8,256,128]{2,3,1,0:T(8,128)S(1)} %get-tuple-element.18, f32[8,8,256,128]{2,3,1,0:T(8,128)S(1)} %get-tuple-element.17, pred[8,8]{1,0:T(8,128)(4,1)S(1)} %fusion.47), kind=kLoop, calls=%fused_computation.2 | loop fusion | flops 12058624 | bytes 18874432 | tf_op jit(solution)/shard_map/while/body/eval_jaxpr/vmap()/reduce_sum | solution.py:92
  78.3 2.3 %convolution_bitcast_fusion.2 = f32[8,128,128]{2,1,0:T(8,128)S(1)} fusion(f32[8,512,128]{1,2,0:T(8,128)S(1)} %fusion, f32[128,256]{1,0:T(8,128)S(1)} %copy-done, f32[128,256]{1,0:T(8,128)S(1)} %copy-done.1), kind=kOutput, calls=%fused_computation.14 | convolution fusion | flops 805437440 | bytes 2883584 | tf_op jit(solution)/shard_map/while/body/eval_jaxpr/vmap()/dot_general | solution.py:93
  80.7 0.8 copy.37
  81.5 4.8 %all-to-all-start.2 = ((f32[2,4,128,128]{3,2,0,1:T(8,128)}), f32[2,4,128,128]{3,2,0,1:T(8,128)S(1)}, u32[]{:S(2)}, u32[]{:S(2)}) async-start(f32[2,4,128,128]{3,2,0,1:T(8,128)} %copy.37), calls=%async_computation.2 | async-start | bytes 1048576 | tf_op jit(solution)/shard_map/all_to_all | solution.py:101
  86.4 1.2 copy.39
  87.8 11.2 %all-to-all-done.2 = f32[2,4,128,128]{3,2,0,1:T(8,128)S(1)} async-done(((f32[2,4,128,128]{3,2,0,1:T(8,128)}), f32[2,4,128,128]{3,2,0,1:T(8,128)S(1)}, u32[]{:S(2)}, u32[]{:S(2)}) %all-to-all-start.2) | async-done | bytes 524320 | tf_op jit(solution)/shard_map/all_to_all | solution.py:101
  99.0 0.3 copy.38
  99.5 4.8 %fusion.1 = bf16[4096,256]{0,1:T(8,128)(2,1)} fusion(bf16[256,512]{1,0:T(8,128)(2,1)S(1)} %fusion.20, bf16[512,4096]{1,0:T(8,128)(2,1)} %param.9), kind=kOutput, calls=%fused_computation.7 | convolution fusion | flops 1074790400 | bytes 6553600 | tf_op jit(solution)/shard_map/dot_general | solution.py:109
  104.3 40.5 %reduce-scatter.2.cloned.1.call-done = bf16[512,256]{0,1:T(8,128)(2,1)} async-done(((bf16[4096,256]{0,1:T(8,128)(2,1)}), bf16[512,256]{0,1:T(8,128)(2,1)}) %reduce-scatter.2.cloned.1.call-update) | async-done | bytes 262160 | tf_op jit(solution)/shard_map/reduce_scatter | solution.py:108
  (41 shorter events, 2.4 us)
Async XLA Ops:
  6.5 18.0 %copy-start.2 = (bf16[7,3,512]{2,0,1:T(8,128)(2,1)S(1)}, bf16[7,3,512]{2,0,1:T(8,128)(2,1)}, u32[]{:S(2)}) copy-start(bf16[7,3,512]{2,0,1:T(8,128)(2,1)} %param.6) | copy-start | bytes 64516
  8.4 33.5 %all-to-all-start = ((bf16[2,1,128,512]{2,0,1,3:T(2,128)(2,1)}), bf16[2,1,128,512]{2,0,1,3:T(2,128)(2,1)S(1)}, u32[]{:S(2)}, u32[]{:S(2)}) async-start(bf16[2,1,128,512]{2,0,1,3:T(2,128)(2,1)} %copy.33), calls=%async_computation | async-start | bytes 524288 | tf_op jit(solution)/shard_map/all_to_all | solution.py:76
  15.7 17.8 %collective-permute-start = (bf16[6,3,512]{0,2,1:T(8,128)(2,1)S(1)}, bf16[6,3,512]{0,2,1:T(8,128)(2,1)S(1)}, u32[]{:S(2)}, u32[]{:S(2)}) collective-permute-start(bf16[6,3,512]{0,2,1:T(8,128)(2,1)S(1)} %bitcast.98), channel_id=1, source_target_pairs={{0,8},{8,16},{16,24},{1,9},{9,17},{17,25},{2,10},{10,18},{18,26},{... | collective-permute-start | bytes 55304 | tf_op jit(solution)/shard_map/ppermute | solution.py:12
  19.9 12.2 %collective-permute-start.1 = (bf16[6,3,512]{0,2,1:T(8,128)(2,1)S(1)}, bf16[6,3,512]{0,2,1:T(8,128)(2,1)}, u32[]{:S(2)}, u32[]{:S(2)}) collective-permute-start(bf16[6,3,512]{0,2,1:T(8,128)(2,1)S(1)} %bitcast.101), channel_id=1, source_target_pairs={{8,0},{16,8},{24,16},{9,1},{17,9},{25,17},{10,2},{18,10},{26,18},{... | collective-permute-start | bytes 55304 | tf_op jit(solution)/shard_map/ppermute | solution.py:12
  41.8 25.0 %all-to-all-start.1 = ((bf16[2,1,128,512]{2,0,1,3:T(2,128)(2,1)}), bf16[2,1,128,512]{2,0,1,3:T(2,128)(2,1)}, u32[]{:S(2)}, u32[]{:S(2)}) async-start(bf16[2,1,128,512]{2,0,1,3:T(2,128)(2,1)} %bitcast.17), calls=%async_computation.1 | async-start | bytes 524288 | tf_op jit(solution)/shard_map/all_to_all | solution.py:75
  76.5 1.8 %copy-start = (f32[128,256]{1,0:T(8,128)S(1)}, f32[128,256]{1,0:T(8,128)}, u32[]{:S(2)}) copy-start(f32[128,256]{1,0:T(8,128)} %slice_negate_fusion) | copy-start | bytes 393220
  76.5 1.8 %copy-start.1 = (f32[128,256]{1,0:T(8,128)S(1)}, f32[128,256]{1,0:T(8,128)}, u32[]{:S(2)}) copy-start(f32[128,256]{1,0:T(8,128)} %slice.208) | copy-start | bytes 393220
  80.5 18.8 %copy-start.3 = (f32[512]{0:T(512)S(1)}, f32[512]{0:T(512)}, u32[]{:S(2)}) copy-start(f32[512]{0:T(512)} %param.8) | copy-start | bytes 6148
  81.5 17.5 %all-to-all-start.2 = ((f32[2,4,128,128]{3,2,0,1:T(8,128)}), f32[2,4,128,128]{3,2,0,1:T(8,128)S(1)}, u32[]{:S(2)}, u32[]{:S(2)}) async-start(f32[2,4,128,128]{3,2,0,1:T(8,128)} %copy.37), calls=%async_computation.2 | async-start | bytes 1048576 | tf_op jit(solution)/shard_map/all_to_all | solution.py:101
  86.4 58.5 %reduce-scatter.2.cloned.1.call-start = ((), (), s32[]{:S(2)}) async-start(), calls=%async_computation.4 | async-start | bytes 2359296 | tf_op jit(solution)/shard_map/reduce_scatter | solution.py:108
Sparse Core Ops, SparseCore 0:
  104.4 40.3 reduce-scatter.1
where the time goes:
time: 152 us
  waiting for transfers between devices  57.4 us (38%)
  other arithmetic  34 us (22%)
  starting transfers between devices  20.6 us (14%)
  local copies, waits for them, and re-layouts  16.8 us (11%)
  between operations  13.7 us (9%)
  matrix products  9.09 us (6%)
    reduce_scatter x1, waiting for transfers between devices, local(): lax.psum_scatter(lax.dot_general(out_weight, token_rows, (((0,), (1,)), (...  40.5 us
    select_n x1, other arithmetic, one_target(): picked = jnp.take(responses, jnp.maximum(distance, 0), axis=0)  12.1 us
    all_to_all x1, waiting for transfers between devices, local(): lax.all_to_all(blocks, 'ctx', split_axis=1, concat_axis=3, tiled=True)  11.2 us
    sub x1, other arithmetic, complex_product(): real_a * real_b - imag_a * imag_b  7.4 us
    gather x1, local copies, waits for them, and re-layouts, one_target(): picked = jnp.take(responses, jnp.maximum(distance, 0), axis=0)  7.37 us
    all_to_all x1, starting transfers between devices, local(): lax.all_to_all(long_filter, 'ctx', split_axis=3, concat_axis=1, tiled=True)  6.32 us
    add x2, other arithmetic, featurize(): summed + kernel[offset].astype(jnp.float32) * extended[margin_rows - offs...  5.91 us
    ppermute x2, waiting for transfers between devices, from_behind(): lax.ppermute(value, axis, [(source, source + steps) for source in range(i...  5.7 us
  transfers between devices with their start and end apart: 6, of which 3 were waited for; matrix products, arithmetic and copies ran while one was open for 25% of the time, Pallas kernels for 0%

commit v1 on v0

--- a/solution.py
+++ b/solution.py
@@ -2,8 +2,439 @@
 
 import jax
 import jax.numpy as jnp
+import ml_dtypes
+import numpy as np
 from jax import lax
+from jax.experimental import pallas as pl
+from jax.experimental.pallas import tpu as pltpu
 from jax.sharding import PartitionSpec as P
+
+F32 = jnp.float32
+BF16 = jnp.bfloat16
+MESH = pl.DeviceIdType.MESH
+RIM = 16
+LANES = 128
+PAIRS = 4
+
+
+def halves(values):
+    high = values.astype(ml_dtypes.bfloat16)
+    low = (values - high.astype(np.float64)).astype(ml_dtypes.bfloat16)
+    return np.stack([high, low])
+
+
+def odd_tables(length):
+    k = np.arange(length)[:, None]
+    t = np.arange(length)[None, :]
+    angles = ((2 * k + 1) * t % (4 * length)) * (np.pi / (2 * length))
+    forward = np.concatenate([np.cos(angles), -np.sin(angles)], axis=0)
+    return halves(forward), halves(forward.T / length)
+
+
+def dot(a, b):
+    return jnp.dot(a, b, preferred_element_type=F32)
+
+
+def kernel(
+    x_ref,
+    taps_ref,
+    filter_ref,
+    skip_ref,
+    weight_hbm,
+    forward_hbm,
+    inverse_hbm,
+    out_ref,
+    weight,
+    forward,
+    inverse,
+    halo,
+    wide,
+    gated,
+    queries,
+    moved,
+    convolved,
+    back,
+    filter_spec,
+    key_spec,
+    own,
+    act,
+    pair_out,
+    pair_in,
+    first_out,
+    first_in,
+    second_out,
+    second_in,
+    local_sem,
+    halo_send,
+    halo_recv,
+    move_send,
+    move_recv,
+    pair_send,
+    pair_recv,
+    first_send,
+    first_recv,
+    second_send,
+    second_recv,
+):
+    rows, channels = gated.shape[1:]
+    taps = taps_ref.shape[0]
+    middle = forward.shape[2]
+    z = lax.axis_index("ctx")
+    ch = lax.axis_index("ch")
+    core, x, y = ch % 2, ch // 2 % 2, ch // 4
+
+    def ch_of(yy, xx, cc):
+        return yy * 4 + xx * 2 + cc
+
+    partner = (z, ch_of(y, x, 1 - core))
+    beside_x = (z, ch_of(y, 1 - x, core))
+    beside_y = (z, ch_of(1 - y, x, core))
+
+    loads = [
+        pltpu.make_async_copy(forward_hbm, forward, local_sem.at[0]),
+        pltpu.make_async_copy(inverse_hbm, inverse, local_sem.at[1]),
+        pltpu.make_async_copy(weight_hbm, weight, local_sem.at[2]),
+    ]
+    for load in loads:
+        load.start()
+
+    barrier = pltpu.get_barrier_semaphore()
+    peers = [((z + o) % PAIRS, ch) for o in range(1, PAIRS)] + [partner, beside_x, beside_y]
+    for peer in peers:
+        pl.semaphore_signal(barrier, inc=1, device_id=peer, device_id_type=MESH)
+    pl.semaphore_wait(barrier, len(peers))
+
+    pending = []
+
+    def remote(src, dst, send, recv, device):
+        return pltpu.make_async_remote_copy(
+            src_ref=src, dst_ref=dst, send_sem=send, recv_sem=recv, device_id=device, device_id_type=MESH
+        )
+
+    last = pl.ds(rows - RIM, RIM)
+    up = remote(x_ref.at[0, :, last], halo.at[0], halo_send.at[0], halo_recv.at[0], ((z + 1) % PAIRS, ch))
+    down = remote(x_ref.at[1, :, last], halo.at[1], halo_send.at[1], halo_recv.at[1], ((z + 3) % PAIRS, ch))
+
+    @pl.when(z < PAIRS - 1)
+    def _():
+        up.start()
+
+    @pl.when(z > 0)
+    def _():
+        down.start()
+
+    def place(h, owner):
+        block = owner if h == 0 else PAIRS - 1 - owner
+        return (
+            pl.ds(pl.multiple_of(block % 2 * rows, rows), rows),
+            pl.ds(pl.multiple_of(block // 2 * LANES, LANES), LANES),
+        )
+
+    def lane_slice(owner):
+        return pl.ds(pl.multiple_of(owner * LANES, LANES), LANES)
+
+    def scatter(kind, source, h):
+        mine_rows, mine_lanes = place(h, z)
+        copies = []
+        for o in (2, 1, 3):
+            target = (z + o) % PAIRS
+            copy = remote(
+                source.at[h, :, lane_slice(target)],
+                moved.at[kind, h, mine_rows, mine_lanes],
+                move_send.at[kind, h, o - 1],
+                move_recv.at[kind, h, o - 1],
+                (target, ch),
+            )
+            copy.start()
+            copies.append(copy)
+        moved[kind, h, mine_rows, mine_lanes] = source[h, :, lane_slice(z)]
+        pending.extend(copies)
+        return copies
+
+    def widen(h):
+        for s in range(3):
+            wide[h, s, RIM:] = x_ref[h, s].astype(F32)
+
+    def taps_of(h, s, cols):
+        total = None
+        for i in range(taps):
+            tap = taps_ref[i].astype(F32)[s : s + 1, cols]
+            term = tap * wide[h, s, pl.ds(RIM - i, rows), cols]
+            total = term if total is None else total + term
+        return total
+
+    columns = [slice(a, a + LANES) for a in range(0, channels, LANES)]
+
+    def make_keys(h):
+        for cols in columns:
+            gated[h, :, cols] = (taps_of(h, 1, cols) * taps_of(h, 2, cols)).astype(BF16)
+
+    def make_queries(h):
+        for cols in columns:
+            queries[h, :, cols] = taps_of(h, 0, cols)
+
+    filter_copies, key_copies = [None, None], [None, None]
+    filter_copies[0] = scatter(0, filter_ref, 0)
+    widen(0)
+    widen(1)
+
+    @pl.when(z > 0)
+    def _():
+        up.wait_recv()
+
+    @pl.when(z == 0)
+    def _():
+        halo[0] = jnp.zeros(halo.shape[1:], BF16)
+
+    for s in range(3):
+        wide[0, s, :RIM] = halo[0, s].astype(F32)
+    make_keys(0)
+    key_copies[0] = scatter(1, gated, 0)
+    filter_copies[1] = scatter(0, filter_ref, 1)
+
+    @pl.when(z < PAIRS - 1)
+    def _():
+        down.wait_recv()
+
+    @pl.when(z == PAIRS - 1)
+    def _():
+        halo[1] = x_ref[0, :, rows - RIM :]
+
+    for s in range(3):
+        wide[1, s, :RIM] = halo[1, s].astype(F32)
+    make_keys(1)
+    key_copies[1] = scatter(1, gated, 1)
+    loads[0].wait()
+
+    signs = (1 - 2 * (lax.broadcasted_iota(jnp.int32, (middle, LANES), 0) % 2)).astype(F32)
+
+    def spectrum(kind, h):
+        data = moved[kind, h]
+        return dot(forward[0], data) + dot(forward[1], data)
+
+    def filter_spectra(h):
+        for copy in filter_copies[h]:
+            copy.wait_recv()
+        both = spectrum(0, h)
+        for m in range(2):
+            filter_spec[0, 2 * h + m] = both[:, m * LANES : (m + 1) * LANES]
+        for b in (2 * h, 2 * h + 1):
+            if b == 0:
+                filter_spec[1, 0] = filter_spec[0, 0]
+            else:
+                filter_spec[1, b, :middle] = filter_spec[0, b, :middle] - signs * filter_spec[0, b - 1, middle:]
+                filter_spec[1, b, middle:] = filter_spec[0, b, middle:] + signs * filter_spec[0, b - 1, :middle]
+
+    def key_spectra(h):
+        for copy in key_copies[h]:
+            copy.wait_recv()
+        both = spectrum(1, h)
+        for m in range(2):
+            key_spec[2 * h + m] = both[:, m * LANES : (m + 1) * LANES]
+
+    def products(i):
+        real, imag = None, None
+        for j in range(i + 1):
+            ra, ia = filter_spec[1, i - j, :middle], filter_spec[1, i - j, middle:]
+            rb, ib = key_spec[j, :middle], key_spec[j, middle:]
+            re, im = ra * rb - ia * ib, ra * ib + ia * rb
+            real = re if real is None else real + re
+            imag = im if imag is None else imag + im
+        return jnp.concatenate([real, imag], axis=0)
+
+    back_copies = [None, None]
+
+    def convolve(h):
+        both = jnp.concatenate([products(2 * h), products(2 * h + 1)], axis=1)
+        high = both.astype(BF16)
+        low = (both - high.astype(F32)).astype(BF16)
+        result = dot(inverse[0], high) + dot(inverse[0], low) + dot(inverse[1], high)
+        convolved[h] = result.astype(BF16)
+        copies = []
+        for o in (2, 1, 3):
+            target = (z + o) % PAIRS
+            its_rows, its_lanes = place(h, target)
+            copy = remote(
+                convolved.at[h, its_rows, its_lanes],
+                back.at[h, :, lane_slice(z)],
+                move_send.at[2, h, o - 1],
+                move_recv.at[2, h, o - 1],
+                (target, ch),
+            )
+            copy.start()
+            copies.append(copy)
+        mine_rows, mine_lanes = place(h, z)
+        back[h, :, lane_slice(z)] = convolved[h, mine_rows, mine_lanes]
+        pending.extend(copies)
+        back_copies[h] = copies
+
+    filter_spectra(0)
+    key_spectra(0)
+    loads[1].wait()
+    convolve(0)
+    make_queries(0)
+    filter_spectra(1)
+    key_spectra(1)
+    convolve(1)
+    make_queries(1)
+    loads[2].wait()
+
+    steps = [(1, 1), (0, 1), (1, 0), (0, 0)]
+    pair_copies = {}
+    half = rows // 2
+    parts = (slice(0, half), slice(half, rows))
+
+    def weights_for(step, cc):
+        yy = 1 - y if step[0] else y
+        xx = 1 - x if step[1] else x
+        return weight[:, pl.ds(pl.multiple_of(ch_of(yy, xx, cc) * channels, channels), channels)]
+
+    def project(h):
+        for copy in back_copies[h]:
+            copy.wait_recv()
+        for cols in columns:
+            summed = back[h, :, cols].astype(F32) + skip_ref[:, cols] * gated[h, :, cols].astype(F32)
+            act[h, :, cols] = (queries[h, :, cols] * summed).astype(BF16)
+        rows_in = act[h]
+        for t, step in enumerate(steps):
+            pair_out[h, t] = dot(rows_in, weights_for(step, 1 - core)).astype(BF16)
+            copy = remote(pair_out.at[h, t], pair_in.at[h, t], pair_send.at[h, t], pair_recv.at[h, t], partner)
+            copy.start()
+            pair_copies[h, t] = copy
+            pending.append(copy)
+        for t, step in enumerate(steps):
+            own[h, t] = dot(rows_in, weights_for(step, core))
+
+    first_copies, second_copies = {}, {}
+
+    def pair_sum(h, t, part):
+        return own[h, t, part] + pair_in[h, t, part].astype(F32)
+
+    def first(h):
+        for t, way, slot in ((0, 0, 0), (0, 1, 0), (1, 0, 1), (2, 1, 1)):
+            if way == 0:
+                pair_copies[h, t].wait_recv()
+            elif t == 2:
+                pair_copies[h, t].wait_recv()
+            first_out[h, way, slot] = pair_sum(h, t, parts[way]).astype(BF16)
+            copy = remote(
+                first_out.at[h, way, slot],
+                first_in.at[h, way, slot],
+                first_send.at[h, way, slot],
+                first_recv.at[h, way, slot],
+                beside_y if way else beside_x,
+            )
+            copy.start()
+            first_copies[h, way, slot] = copy
+            pending.append(copy)
+
+    def second(h):
+        for way in range(2):
+            first_copies[h, way, 0].wait_recv()
+            t = 1 if way else 2
+            total = pair_sum(h, t, parts[way]) + first_in[h, way, 0].astype(F32)
+            second_out[h, way] = total.astype(BF16)
+            copy = remote(
+                second_out.at[h, way],
+                second_in.at[h, way],
+                second_send.at[h, way],
+                second_recv.at[h, way],
+                beside_x if way else beside_y,
+            )
+            copy.start()
+            second_copies[h, way] = copy
+            pending.append(copy)
+
+    def finish(h):
+        pair_copies[h, 3].wait_recv()
+        for way in range(2):
+            first_copies[h, way, 1].wait_recv()
+            total = pair_sum(h, 3, parts[way]) + first_in[h, way, 1].astype(F32)
+            second_copies[h, way].wait_recv()
+            out_ref[h, parts[way]] = (total + second_in[h, way].astype(F32)).astype(BF16)
+
+    project(0)
+    first(0)
+    project(1)
+    second(0)
+    first(1)
+    finish(0)
+    second(1)
+    finish(1)
+
+    @pl.when(z < PAIRS - 1)
+    def _():
+        up.wait_send()
+
+    @pl.when(z > 0)
+    def _():
+        down.wait_send()
+
+    for copy in pending:
+        copy.wait_send()
+
+
+def fused(features, short_weight, long_filter, skip_gain, out_weight):
+    rows, channels = long_filter.shape[2:]
+    middle = 2 * rows
+    streams = jnp.transpose(features[:, 0], (0, 2, 1, 3))
+    forward, inverse = odd_tables(middle)
+    in_vmem = pl.BlockSpec(memory_space=pltpu.VMEM)
+    in_hbm = pl.BlockSpec(memory_space=pl.ANY)
+    vmem = pltpu.VMEM
+    dma = pltpu.SemaphoreType.DMA
+    out = pl.pallas_call(
+        kernel,
+        out_shape=jax.ShapeDtypeStruct((2, rows, channels), BF16),
+        in_specs=[in_vmem] * 4 + [in_hbm] * 3,
+        out_specs=in_vmem,
+        scratch_shapes=[
+            vmem(out_weight.shape, BF16),
+            vmem(forward.shape, BF16),
+            vmem(inverse.shape, BF16),
+            vmem((2, 3, RIM, channels), BF16),
+            vmem((2, 3, RIM + rows, channels), F32),
+            vmem((2, rows, channels), BF16),
+            vmem((2, rows, channels), F32),
+            vmem((2, 2, middle, 2 * LANES), BF16),
+            vmem((2, middle, 2 * LANES), BF16),
+            vmem((2, rows, channels), BF16),
+            vmem((2, 4, 2 * middle, LANES), F32),
+            vmem((4, 2 * middle, LANES), F32),
+            vmem((2, 4, rows, channels), F32),
+            vmem((2, rows, channels), BF16),
+            vmem((2, 4, rows, channels), BF16),
+            vmem((2, 4, rows, channels), BF16),
+            vmem((2, 2, 2, rows // 2, channels), BF16),
+            vmem((2, 2, 2, rows // 2, channels), BF16),
+            vmem((2, 2, rows // 2, channels), BF16),
+            vmem((2, 2, rows // 2, channels), BF16),
+            dma((3,)),
+            dma((2,)),
+            dma((2,)),
+            dma((3, 2, 3)),
+            dma((3, 2, 3)),
+            dma((2, 4)),
+            dma((2, 4)),
+            dma((2, 2, 2)),
+            dma((2, 2, 2)),
+            dma((2, 2)),
+            dma((2, 2)),
+        ],
+        compiler_params=pltpu.CompilerParams(
+            collective_id=0, has_side_effects=True, vmem_limit_bytes=48 * 1024 * 1024
+        ),
+        name="hyena",
+    )(
+        streams,
+        short_weight,
+        long_filter[:, 0],
+        skip_gain.reshape(1, channels),
+        out_weight,
+        jnp.asarray(forward),
+        jnp.asarray(inverse),
+    )
+    return out[:, None]
 
 
 def from_behind(value, axis, steps):
@@ -126,4 +557,7 @@
         P("ch", None),
     )
     out_specs = P(None, "ctx", None, "ch")
-    return jax.shard_map(local, mesh=mesh, in_specs=in_specs, out_specs=out_specs, check_vma=False)
+    shape = dict(mesh.shape)
+    suits = shape == {"ctx": PAIRS, "ch": 8}
+    body = fused if suits else local
+    return jax.shard_map(body, mesh=mesh, in_specs=in_specs, out_specs=out_specs, check_vma=False)

time: 152 us -> 44 us (0.29)
  waiting for transfers between devices: 57.4 us -> 0 us
  Pallas kernels: 0 us -> 37.3 us
  other arithmetic: 34 us -> 0 us
  starting transfers between devices: 20.6 us -> 0 us
  between operations: 13.7 us -> 0.02 us
  local copies, waits for them, and re-layouts: 16.8 us -> 6.3 us
  matrix products: 9.09 us -> 0 us
    reduce_scatter x1 -> x0, waiting for transfers between devices: 40.5 us -> none  [local(): lax.psum_scatter(lax.dot_general(out_weight, token_rows, (((0,), (1,)), (...]
    pallas_call x0 -> x1, Pallas kernels: none -> 37.3 us  [fused(): pl.pallas_call(kernel, out_shape=jax.ShapeDtypeStruct((2, rows, channels)...]
    all_to_all x3 -> x0, starting transfers between devices: 15.4 us -> none  [the longest x1 6.32 us: local(): lax.all_to_all(long_filter, 'ctx', split_axis=3, concat_axis=1, tiled=True)]
    select_n x2 -> x0, other arithmetic: 13.2 us -> none  [the longest x1 12.1 us: one_target(): picked = jnp.take(responses, jnp.maximum(distance, 0), axis=0)]
    all_to_all x3 -> x0, waiting for transfers between devices: 11.2 us -> none  [the longest x1 11.2 us: local(): lax.all_to_all(blocks, 'ctx', split_axis=1, concat_axis=3, tiled=True)]
    dot_general x4 -> x0, matrix products: 9.09 us -> none  [the longest x1 4.78 us: local(): lax.dot_general(out_weight, token_rows, (((0,), (1,)), ((), ())), preferr...]
    sub x1 -> x0, other arithmetic: 7.4 us -> none  [complex_product(): real_a * real_b - imag_a * imag_b]
    gather x1 -> x0, local copies, waits for them, and re-layouts: 7.37 us -> none  [one_target(): picked = jnp.take(responses, jnp.maximum(distance, 0), axis=0)]
  transfers between devices with their start and end apart: 6 -> 0, of which waited for: 3 -> 0; matrix products, arithmetic and copies ran while one was open for 25% -> 0% of each run, Pallas kernels for 0% -> 0%
where the time goes in v1:
time: 44 us; the launch traced here: 43.7 us
  Pallas kernels  37.3 us (85%)
  local copies, waits for them, and re-layouts  6.3 us (14%)
    pallas_call x1, Pallas kernels, fused(): pl.pallas_call(kernel, out_shape=jax.ShapeDtypeStruct((2, rows, channels)...  37.3 us
    unnamed x12, local copies, waits for them, and re-layouts  6.3 us

profile of v1, /device:TPU:0, one launch (start us, length us, event | category | flops | bytes accessed | tf_op | source)
XLA Modules:
  0.0 43.7 jit_solution(10046547486554727653)
XLA Ops:
  0.0 0.8 %copy.8.taps_ref = bf16[7,3,512]{2,1,0:T(4,128)(2,1)S(1)} copy(bf16[7,3,512]{2,0,1:T(8,128)(2,1)} %param.8) | data formatting | bytes 43008 | tf_op args[1]
  0.8 0.0 copy-start
  0.8 1.1 %copy-done = bf16[2,1,128,3,512]{4,2,3,1,0:T(8,128)(2,1)S(1)} copy-done((bf16[2,1,128,3,512]{4,2,3,1,0:T(8,128)(2,1)S(1)}, bf16[2,1,128,3,512]{4,2,3,1,0:T(8,128)(2,1)}, u32[]{:S(2)}) %copy-start) | copy-done | bytes 786456
  1.9 0.0 copy-start.1
  1.9 1.0 %copy-done.1 = bf16[2,256,512]{2,1,0:T(8,128)(2,1)S(1)} copy-done((bf16[2,256,512]{2,1,0:T(8,128)(2,1)S(1)}, bf16[2,256,512]{2,1,0:T(8,128)(2,1)}, u32[]{:S(2)}) %copy-start.1) | copy-done | bytes 524312
  2.9 0.0 copy-start.2
  2.9 1.0 %copy-done.2 = bf16[2,512,256]{2,1,0:T(8,128)(2,1)S(1)} copy-done((bf16[2,512,256]{2,1,0:T(8,128)(2,1)S(1)}, bf16[2,512,256]{2,1,0:T(8,128)(2,1)}, u32[]{:S(2)}) %copy-start.2) | copy-done | bytes 524312
  4.0 0.0 copy-start.3
  4.0 0.9 %copy-done.3 = bf16[2,1,128,512]{3,2,1,0:T(8,128)(2,1)S(1)} copy-done((bf16[2,1,128,512]{3,2,1,0:T(8,128)(2,1)S(1)}, bf16[2,1,128,512]{3,2,1,0:T(8,128)(2,1)}, u32[]{:S(2)}) %copy-start.3) | copy-done | bytes 262168
  4.9 0.0 copy-start.4
  4.9 0.7 %copy-done.4 = f32[512]{0:T(512)S(1)} copy-done((f32[512]{0:T(512)S(1)}, f32[512]{0:T(512)}, u32[]{:S(2)}) %copy-start.4) | copy-done | bytes 2072
  5.6 37.3 %hyena.1 = bf16[2,128,512]{2,1,0:T(8,128)(2,1)S(1)} custom-call(bf16[2,3,128,512]{3,2,1,0:T(8,128)(2,1)S(1)} %bitcast.9, bf16[7,3,512]{2,1,0:T(4,128)(2,1)S(1)} %copy.8.taps_ref, bf16[2,128,512]{2,1,0:T(8,128)(2,1)S(1)} %bitcast.10, f32[1,512]{1,0:T(1,128)S(1)} %bitcast.11, bf16[512,4096]{1,0:T(8,128)(2,1)} %weight_hbm.1, ...), custom_call_target="tpu_custom_call" | custom-call | tf_op jit(solution)/shard_map/hyena/pallas_call | solution.py:386
  43.0 0.7 %copy.11 = bf16[2,1,128,512]{3,2,1,0:T(8,128)(2,1)} copy(bf16[2,1,128,512]{3,2,1,0:T(8,128)(2,1)S(1)} %bitcast.8) | data formatting | bytes 524288
Async XLA Ops:
  0.8 1.1 %copy-start = (bf16[2,1,128,3,512]{4,2,3,1,0:T(8,128)(2,1)S(1)}, bf16[2,1,128,3,512]{4,2,3,1,0:T(8,128)(2,1)}, u32[]{:S(2)}) copy-start(bf16[2,1,128,3,512]{4,2,3,1,0:T(8,128)(2,1)} %param.7) | copy-start | bytes 2359300
  1.9 1.0 %copy-start.1 = (bf16[2,256,512]{2,1,0:T(8,128)(2,1)S(1)}, bf16[2,256,512]{2,1,0:T(8,128)(2,1)}, u32[]{:S(2)}) copy-start(bf16[2,256,512]{2,1,0:T(8,128)(2,1)} %constant.5.clone.inverse_hbm) | copy-start | bytes 1572868
  2.9 1.0 %copy-start.2 = (bf16[2,512,256]{2,1,0:T(8,128)(2,1)S(1)}, bf16[2,512,256]{2,1,0:T(8,128)(2,1)}, u32[]{:S(2)}) copy-start(bf16[2,512,256]{2,1,0:T(8,128)(2,1)} %constant.4.clone.forward_hbm) | copy-start | bytes 1572868
  4.0 0.9 %copy-start.3 = (bf16[2,1,128,512]{3,2,1,0:T(8,128)(2,1)S(1)}, bf16[2,1,128,512]{3,2,1,0:T(8,128)(2,1)}, u32[]{:S(2)}) copy-start(bf16[2,1,128,512]{3,2,1,0:T(8,128)(2,1)} %param.9) | copy-start | bytes 786436
  4.9 0.7 %copy-start.4 = (f32[512]{0:T(512)S(1)}, f32[512]{0:T(512)}, u32[]{:S(2)}) copy-start(f32[512]{0:T(512)} %param.10) | copy-start | bytes 6148

commit v2 on v1

--- a/solution.py
+++ b/solution.py
@@ -36,14 +36,18 @@
 
 
 def kernel(
+    x_hbm,
+    taps_hbm,
+    filter_hbm,
+    skip_hbm,
+    weight_hbm,
+    forward_hbm,
+    inverse_hbm,
+    out_ref,
     x_ref,
     taps_ref,
     filter_ref,
     skip_ref,
-    weight_hbm,
-    forward_hbm,
-    inverse_hbm,
-    out_ref,
     weight,
     forward,
     inverse,
@@ -77,7 +81,7 @@
     second_recv,
 ):
     rows, channels = gated.shape[1:]
-    taps = taps_ref.shape[0]
+    taps = taps_ref.shape[1]
     middle = forward.shape[2]
     z = lax.axis_index("ctx")
     ch = lax.axis_index("ch")
@@ -90,12 +94,13 @@
     beside_x = (z, ch_of(y, 1 - x, core))
     beside_y = (z, ch_of(1 - y, x, core))
 
+    sources = (x_hbm, filter_hbm, taps_hbm, skip_hbm, forward_hbm, inverse_hbm, weight_hbm)
+    places = (x_ref, filter_ref, taps_ref, skip_ref, forward, inverse, weight)
     loads = [
-        pltpu.make_async_copy(forward_hbm, forward, local_sem.at[0]),
-        pltpu.make_async_copy(inverse_hbm, inverse, local_sem.at[1]),
-        pltpu.make_async_copy(weight_hbm, weight, local_sem.at[2]),
+        pltpu.make_async_copy(source, target, local_sem.at[i])
+        for i, (source, target) in enumerate(zip(sources, places))
     ]
-    for load in loads:
+    for load in loads[:4]:
         load.start()
 
     barrier = pltpu.get_barrier_semaphore()
@@ -104,6 +109,10 @@
         pl.semaphore_signal(barrier, inc=1, device_id=peer, device_id_type=MESH)
     pl.semaphore_wait(barrier, len(peers))
 
+    for load in loads[4:]:
+        load.start()
+    for load in loads[:4]:
+        load.wait()
     pending = []
 
     def remote(src, dst, send, recv, device):
@@ -158,7 +167,7 @@
     def taps_of(h, s, cols):
         total = None
         for i in range(taps):
-            tap = taps_ref[i].astype(F32)[s : s + 1, cols]
+            tap = taps_ref[s].astype(F32)[i : i + 1, cols]
             term = tap * wide[h, s, pl.ds(RIM - i, rows), cols]
             total = term if total is None else total + term
         return total
@@ -204,7 +213,7 @@
         wide[1, s, :RIM] = halo[1, s].astype(F32)
     make_keys(1)
     key_copies[1] = scatter(1, gated, 1)
-    loads[0].wait()
+    loads[4].wait()
 
     signs = (1 - 2 * (lax.broadcasted_iota(jnp.int32, (middle, LANES), 0) % 2)).astype(F32)
 
@@ -270,14 +279,14 @@
 
     filter_spectra(0)
     key_spectra(0)
-    loads[1].wait()
+    loads[5].wait()
     convolve(0)
     make_queries(0)
     filter_spectra(1)
     key_spectra(1)
     convolve(1)
     make_queries(1)
-    loads[2].wait()
+    loads[6].wait()
 
     steps = [(1, 1), (0, 1), (1, 0), (0, 0)]
     pair_copies = {}
@@ -378,6 +387,7 @@
     rows, channels = long_filter.shape[2:]
     middle = 2 * rows
     streams = jnp.transpose(features[:, 0], (0, 2, 1, 3))
+    taps = jnp.transpose(short_weight, (1, 0, 2))
     forward, inverse = odd_tables(middle)
     in_vmem = pl.BlockSpec(memory_space=pltpu.VMEM)
     in_hbm = pl.BlockSpec(memory_space=pl.ANY)
@@ -386,9 +396,13 @@
     out = pl.pallas_call(
         kernel,
         out_shape=jax.ShapeDtypeStruct((2, rows, channels), BF16),
-        in_specs=[in_vmem] * 4 + [in_hbm] * 3,
+        in_specs=[in_hbm] * 7,
         out_specs=in_vmem,
         scratch_shapes=[
+            vmem(streams.shape, BF16),
+            vmem(taps.shape, BF16),
+            vmem((2, rows, channels), BF16),
+            vmem((1, channels), F32),
             vmem(out_weight.shape, BF16),
             vmem(forward.shape, BF16),
             vmem(inverse.shape, BF16),
@@ -409,7 +423,7 @@
             vmem((2, 2, 2, rows // 2, channels), BF16),
             vmem((2, 2, rows // 2, channels), BF16),
             vmem((2, 2, rows // 2, channels), BF16),
-            dma((3,)),
+            dma((7,)),
             dma((2,)),
             dma((2,)),
             dma((3, 2, 3)),
@@ -422,12 +436,12 @@
             dma((2, 2)),
         ],
         compiler_params=pltpu.CompilerParams(
-            collective_id=0, has_side_effects=True, vmem_limit_bytes=48 * 1024 * 1024
+            collective_id=0, has_side_effects=True, vmem_limit_bytes=62 * 1024 * 1024
         ),
         name="hyena",
     )(
         streams,
-        short_weight,
+        taps,
         long_filter[:, 0],
         skip_gain.reshape(1, channels),
         out_weight,

time: 44 us -> 39.8 us (0.905)
  local copies, waits for them, and re-layouts: 6.3 us -> 1.67 us
  Pallas kernels: 37.3 us -> 38 us
    unnamed x12 -> x1, local copies, waits for them, and re-layouts: 6.3 us -> 1.67 us
    pallas_call x1, Pallas kernels: 37.3 us -> 38 us  [fused(): pl.pallas_call(kernel, out_shape=jax.ShapeDtypeStruct((2, rows, channels)...]
where the time goes in v2:
time: 39.8 us; the launch traced here: 39.7 us
  Pallas kernels  38 us (95%)
  local copies, waits for them, and re-layouts  1.67 us (4%)
    pallas_call x1, Pallas kernels, fused(): pl.pallas_call(kernel, out_shape=jax.ShapeDtypeStruct((2, rows, channels)...  38 us
    unnamed x1, local copies, waits for them, and re-layouts  1.67 us

profile of v2, /device:TPU:0, one launch (start us, length us, event | category | flops | bytes accessed | tf_op | source)
XLA Modules:
  0.0 39.7 jit_solution(7319135477813237282)
XLA Ops:
  0.0 38.0 %hyena.1 = bf16[2,128,512]{2,1,0:T(8,128)(2,1)} custom-call(bf16[2,3,128,512]{3,2,1,0:T(8,128)(2,1)} %bitcast.10, bf16[3,7,512]{2,1,0:T(8,128)(2,1)} %bitcast.12, bf16[2,128,512]{2,1,0:T(8,128)(2,1)} %bitcast.11, f32[1,512]{1,0:T(1,128)} %bitcast.13, bf16[512,4096]{1,0:T(8,128)(2,1)} %weight_hbm.1, bf16[2,512,256]{2,1,0:T(8,128)(2,1)} %constant.4.clone.forward_hbm, ...), custom_call_target="tpu_custom_call" | custom-call | tf_op jit(solution)/shard_map/hyena/pallas_call | solution.py:396
  38.0 1.7 %copy.10 = bf16[2,1,128,512]{3,2,1,0:T(8,128)(2,1)} copy(bf16[2,1,128,512]{3,2,1,0:T(8,128)(2,1)} %bitcast.9) | data formatting | bytes 524288

commit v3 on v2

--- a/solution.py
+++ b/solution.py
@@ -12,7 +12,8 @@
 F32 = jnp.float32
 BF16 = jnp.bfloat16
 MESH = pl.DeviceIdType.MESH
-RIM = 16
+RIM = 8
+STRIP = 64
 LANES = 128
 PAIRS = 4
 
@@ -51,6 +52,7 @@
     weight,
     forward,
     inverse,
+    rim_out,
     halo,
     wide,
     gated,
@@ -60,6 +62,7 @@
     back,
     filter_spec,
     key_spec,
+    summed_spec,
     own,
     act,
     pair_out,
@@ -73,6 +76,8 @@
     halo_recv,
     move_send,
     move_recv,
+    back_send,
+    back_recv,
     pair_send,
     pair_recv,
     first_send,
@@ -120,22 +125,56 @@
             src_ref=src, dst_ref=dst, send_sem=send, recv_sem=recv, device_id=device, device_id_type=MESH
         )
 
-    last = pl.ds(rows - RIM, RIM)
-    up = remote(x_ref.at[0, :, last], halo.at[0], halo_send.at[0], halo_recv.at[0], ((z + 1) % PAIRS, ch))
-    down = remote(x_ref.at[1, :, last], halo.at[1], halo_send.at[1], halo_recv.at[1], ((z + 3) % PAIRS, ch))
-
-    @pl.when(z < PAIRS - 1)
-    def _():
-        up.start()
-
-    @pl.when(z > 0)
-    def _():
-        down.start()
-
-    def place(h, owner):
+    def widen(h):
+        for s in range(3):
+            wide[h, s, RIM:] = x_ref[h, s].astype(F32)
+
+    widen(0)
+    widen(1)
+    tail = slice(rows, rows + RIM)
+    rims = {}
+    for kind, streams in ((0, (1, 2)), (1, (0, 0))):
+        for h in range(2):
+            rim_out[kind, h] = jnp.concatenate([wide[h, s, tail] for s in streams], axis=0).astype(BF16)
+            rims[kind, h] = remote(
+                rim_out.at[kind, h],
+                halo.at[kind, h],
+                halo_send.at[kind, h],
+                halo_recv.at[kind, h],
+                ((z + (1 if h == 0 else 3)) % PAIRS, ch),
+            )
+
+    def send_rims(kind):
+        @pl.when(z < PAIRS - 1)
+        def _():
+            rims[kind, 0].start()
+
+        @pl.when(z > 0)
+        def _():
+            rims[kind, 1].start()
+
+    def take_rim(kind, h):
+        has = z > 0 if h == 0 else z < PAIRS - 1
+
+        @pl.when(has)
+        def _():
+            rims[kind, h].wait_recv()
+
+        @pl.when(jnp.logical_not(has))
+        def _():
+            halo[kind, h] = jnp.zeros(halo.shape[2:], BF16) if h == 0 else rim_out[kind, 0]
+
+        both = halo[kind, h].astype(F32)
+        for m, s in enumerate((1, 2) if kind == 0 else (0,)):
+            wide[h, s, :RIM] = both[m * RIM : (m + 1) * RIM]
+
+    send_rims(0)
+
+    def place(h, owner, first_row=0, count=None):
         block = owner if h == 0 else PAIRS - 1 - owner
+        count = rows if count is None else count
         return (
-            pl.ds(pl.multiple_of(block % 2 * rows, rows), rows),
+            pl.ds(pl.multiple_of(block % 2 * rows + first_row, count), count),
             pl.ds(pl.multiple_of(block // 2 * LANES, LANES), LANES),
         )
 
@@ -160,14 +199,12 @@
         pending.extend(copies)
         return copies
 
-    def widen(h):
-        for s in range(3):
-            wide[h, s, RIM:] = x_ref[h, s].astype(F32)
+    tap_rows = [taps_ref[s].astype(F32) for s in range(3)]
 
     def taps_of(h, s, cols):
         total = None
         for i in range(taps):
-            tap = taps_ref[s].astype(F32)[i : i + 1, cols]
+            tap = tap_rows[s][i : i + 1, cols]
             term = tap * wide[h, s, pl.ds(RIM - i, rows), cols]
             total = term if total is None else total + term
         return total
@@ -184,35 +221,13 @@
 
     filter_copies, key_copies = [None, None], [None, None]
     filter_copies[0] = scatter(0, filter_ref, 0)
-    widen(0)
-    widen(1)
-
-    @pl.when(z > 0)
-    def _():
-        up.wait_recv()
-
-    @pl.when(z == 0)
-    def _():
-        halo[0] = jnp.zeros(halo.shape[1:], BF16)
-
-    for s in range(3):
-        wide[0, s, :RIM] = halo[0, s].astype(F32)
+    take_rim(0, 0)
     make_keys(0)
     key_copies[0] = scatter(1, gated, 0)
+    send_rims(1)
     filter_copies[1] = scatter(0, filter_ref, 1)
-
-    @pl.when(z < PAIRS - 1)
-    def _():
-        down.wait_recv()
-
-    @pl.when(z == PAIRS - 1)
-    def _():
-        halo[1] = x_ref[0, :, rows - RIM :]
-
-    for s in range(3):
-        wide[1, s, :RIM] = halo[1, s].astype(F32)
+    take_rim(0, 1)
     make_keys(1)
-    key_copies[1] = scatter(1, gated, 1)
     loads[4].wait()
 
     signs = (1 - 2 * (lax.broadcasted_iota(jnp.int32, (middle, LANES), 0) % 2)).astype(F32)
@@ -241,143 +256,183 @@
         for m in range(2):
             key_spec[2 * h + m] = both[:, m * LANES : (m + 1) * LANES]
 
-    def products(i):
-        real, imag = None, None
-        for j in range(i + 1):
-            ra, ia = filter_spec[1, i - j, :middle], filter_spec[1, i - j, middle:]
-            rb, ib = key_spec[j, :middle], key_spec[j, middle:]
-            re, im = ra * rb - ia * ib, ra * ib + ia * rb
-            real = re if real is None else real + re
-            imag = im if imag is None else imag + im
-        return jnp.concatenate([real, imag], axis=0)
-
-    back_copies = [None, None]
-
-    def convolve(h):
-        both = jnp.concatenate([products(2 * h), products(2 * h + 1)], axis=1)
-        high = both.astype(BF16)
-        low = (both - high.astype(F32)).astype(BF16)
-        result = dot(inverse[0], high) + dot(inverse[0], low) + dot(inverse[1], high)
-        convolved[h] = result.astype(BF16)
+    def products(h):
+        for m in range(2):
+            i = 2 * h + m
+            cols = slice(m * LANES, (m + 1) * LANES)
+            for start in range(0, middle, STRIP):
+                re_rows = slice(start, start + STRIP)
+                im_rows = slice(middle + start, middle + start + STRIP)
+                real, imag = None, None
+                for j in range(i + 1):
+                    ra, ia = filter_spec[1, i - j, re_rows], filter_spec[1, i - j, im_rows]
+                    rb, ib = key_spec[j, re_rows], key_spec[j, im_rows]
+                    re, im = ra * rb - ia * ib, ra * ib + ia * rb
+                    real = re if real is None else real + re
+                    imag = im if imag is None else imag + im
+                for where, value in ((re_rows, real), (im_rows, imag)):
+                    high = value.astype(BF16)
+                    summed_spec[0, where, cols] = high
+                    summed_spec[1, where, cols] = (value - high.astype(F32)).astype(BF16)
+
+    chunks = [(0, 0, rows), (1, 0, rows // 2), (1, rows // 2, rows // 2)]
+    back_copies = {}
+
+    def send_back(q):
+        h, first_row, count = chunks[q]
         copies = []
         for o in (2, 1, 3):
             target = (z + o) % PAIRS
-            its_rows, its_lanes = place(h, target)
+            its_rows, its_lanes = place(h, target, first_row, count)
             copy = remote(
                 convolved.at[h, its_rows, its_lanes],
-                back.at[h, :, lane_slice(z)],
-                move_send.at[2, h, o - 1],
-                move_recv.at[2, h, o - 1],
+                back.at[h, pl.ds(first_row, count), lane_slice(z)],
+                back_send.at[q, o - 1],
+                back_recv.at[q, o - 1],
                 (target, ch),
             )
             copy.start()
             copies.append(copy)
-        mine_rows, mine_lanes = place(h, z)
-        back[h, :, lane_slice(z)] = convolved[h, mine_rows, mine_lanes]
+        mine_rows, mine_lanes = place(h, z, first_row, count)
+        back[h, pl.ds(first_row, count), lane_slice(z)] = convolved[h, mine_rows, mine_lanes]
         pending.extend(copies)
-        back_copies[h] = copies
+        back_copies[q] = copies
+
+    def convolve(h):
+        products(h)
+        high, low = summed_spec[0], summed_spec[1]
+        result = dot(inverse[0], high) + dot(inverse[0], low) + dot(inverse[1], high)
+        convolved[h] = result.astype(BF16)
 
     filter_spectra(0)
     key_spectra(0)
+    key_copies[1] = scatter(1, gated, 1)
     loads[5].wait()
     convolve(0)
+    send_back(0)
+    take_rim(1, 0)
     make_queries(0)
+    take_rim(1, 1)
+    make_queries(1)
     filter_spectra(1)
     key_spectra(1)
     convolve(1)
-    make_queries(1)
+    send_back(1)
+    send_back(2)
     loads[6].wait()
 
     steps = [(1, 1), (0, 1), (1, 0), (0, 0)]
     pair_copies = {}
-    half = rows // 2
-    parts = (slice(0, half), slice(half, rows))
+
+    def parts(q):
+        h, first_row, count = chunks[q]
+        half = count // 2
+        return slice(first_row, first_row + half), slice(first_row + half, first_row + count)
+
+    def slot_rows(q):
+        return pl.ds(chunks[q][1] // 2, chunks[q][2] // 2)
 
     def weights_for(step, cc):
         yy = 1 - y if step[0] else y
         xx = 1 - x if step[1] else x
         return weight[:, pl.ds(pl.multiple_of(ch_of(yy, xx, cc) * channels, channels), channels)]
 
-    def project(h):
-        for copy in back_copies[h]:
+    def project(q):
+        h, first_row, count = chunks[q]
+        span = slice(first_row, first_row + count)
+        for copy in back_copies[q]:
             copy.wait_recv()
         for cols in columns:
-            summed = back[h, :, cols].astype(F32) + skip_ref[:, cols] * gated[h, :, cols].astype(F32)
-            act[h, :, cols] = (queries[h, :, cols] * summed).astype(BF16)
-        rows_in = act[h]
+            summed = back[h, span, cols].astype(F32) + skip_ref[:, cols] * gated[h, span, cols].astype(F32)
+            act[h, span, cols] = (queries[h, span, cols] * summed).astype(BF16)
+        rows_in = act[h, span]
         for t, step in enumerate(steps):
-            pair_out[h, t] = dot(rows_in, weights_for(step, 1 - core)).astype(BF16)
-            copy = remote(pair_out.at[h, t], pair_in.at[h, t], pair_send.at[h, t], pair_recv.at[h, t], partner)
+            pair_out[h, t, span] = dot(rows_in, weights_for(step, 1 - core)).astype(BF16)
+            copy = remote(
+                pair_out.at[h, t, pl.ds(first_row, count)],
+                pair_in.at[h, t, pl.ds(first_row, count)],
+                pair_send.at[q, t],
+                pair_recv.at[q, t],
+                partner,
+            )
             copy.start()
-            pair_copies[h, t] = copy
+            pair_copies[q, t] = copy
             pending.append(copy)
         for t, step in enumerate(steps):
-            own[h, t] = dot(rows_in, weights_for(step, core))
+            own[h, t, span] = dot(rows_in, weights_for(step, core))
 
     first_copies, second_copies = {}, {}
 
-    def pair_sum(h, t, part):
+    def pair_sum(q, t, way):
+        h, part = chunks[q][0], parts(q)[way]
         return own[h, t, part] + pair_in[h, t, part].astype(F32)
 
-    def first(h):
+    def first(q):
+        h, where = chunks[q][0], slot_rows(q)
         for t, way, slot in ((0, 0, 0), (0, 1, 0), (1, 0, 1), (2, 1, 1)):
-            if way == 0:
-                pair_copies[h, t].wait_recv()
-            elif t == 2:
-                pair_copies[h, t].wait_recv()
-            first_out[h, way, slot] = pair_sum(h, t, parts[way]).astype(BF16)
+            if (t, way) != (0, 1):
+                pair_copies[q, t].wait_recv()
+            first_out[h, way, slot, where] = pair_sum(q, t, way).astype(BF16)
             copy = remote(
-                first_out.at[h, way, slot],
-                first_in.at[h, way, slot],
-                first_send.at[h, way, slot],
-                first_recv.at[h, way, slot],
+                first_out.at[h, way, slot, where],
+                first_in.at[h, way, slot, where],
+                first_send.at[q, way, slot],
+                first_recv.at[q, way, slot],
                 beside_y if way else beside_x,
             )
             copy.start()
-            first_copies[h, way, slot] = copy
+            first_copies[q, way, slot] = copy
             pending.append(copy)
 
-    def second(h):
+    def second(q):
+        h, where = chunks[q][0], slot_rows(q)
         for way in range(2):
-            first_copies[h, way, 0].wait_recv()
+            first_copies[q, way, 0].wait_recv()
             t = 1 if way else 2
-            total = pair_sum(h, t, parts[way]) + first_in[h, way, 0].astype(F32)
-            second_out[h, way] = total.astype(BF16)
+            total = pair_sum(q, t, way) + first_in[h, way, 0, where].astype(F32)
+            second_out[h, way, where] = total.astype(BF16)
             copy = remote(
-                second_out.at[h, way],
-                second_in.at[h, way],
-                second_send.at[h, way],
-                second_recv.at[h, way],
+                second_out.at[h, way, where],
+                second_in.at[h, way, where],
+                second_send.at[q, way],
+                second_recv.at[q, way],
                 beside_x if way else beside_y,
             )
             copy.start()
-            second_copies[h, way] = copy
+            second_copies[q, way] = copy
             pending.append(copy)
 
-    def finish(h):
-        pair_copies[h, 3].wait_recv()
+    def finish(q):
+        h, where = chunks[q][0], slot_rows(q)
+        pair_copies[q, 3].wait_recv()
         for way in range(2):
-            first_copies[h, way, 1].wait_recv()
-            total = pair_sum(h, 3, parts[way]) + first_in[h, way, 1].astype(F32)
-            second_copies[h, way].wait_recv()
-            out_ref[h, parts[way]] = (total + second_in[h, way].astype(F32)).astype(BF16)
+            first_copies[q, way, 1].wait_recv()
+            total = pair_sum(q, 3, way) + first_in[h, way, 1, where].astype(F32)
+            second_copies[q, way].wait_recv()
+            out_ref[h, parts(q)[way]] = (total + second_in[h, way, where].astype(F32)).astype(BF16)
 
     project(0)
     first(0)
     project(1)
+    first(1)
+    project(2)
     second(0)
-    first(1)
+    first(2)
+    second(1)
     finish(0)
-    second(1)
+    second(2)
     finish(1)
+    finish(2)
 
     @pl.when(z < PAIRS - 1)
     def _():
-        up.wait_send()
+        rims[0, 0].wait_send()
+        rims[1, 0].wait_send()
 
     @pl.when(z > 0)
     def _():
-        down.wait_send()
+        rims[0, 1].wait_send()
+        rims[1, 1].wait_send()
 
     for copy in pending:
         copy.wait_send()
@@ -395,7 +450,7 @@
     dma = pltpu.SemaphoreType.DMA
     out = pl.pallas_call(
         kernel,
-        out_shape=jax.ShapeDtypeStruct((2, rows, channels), BF16),
+        out_shape=pltpu.VMEM((2, rows, channels), BF16),
         in_specs=[in_hbm] * 7,
         out_specs=in_vmem,
         scratch_shapes=[
@@ -406,7 +461,8 @@
             vmem(out_weight.shape, BF16),
             vmem(forward.shape, BF16),
             vmem(inverse.shape, BF16),
-            vmem((2, 3, RIM, channels), BF16),
+            vmem((2, 2, 2 * RIM, channels), BF16),
+            vmem((2, 2, 2 * RIM, channels), BF16),
             vmem((2, 3, RIM + rows, channels), F32),
             vmem((2, rows, channels), BF16),
             vmem((2, rows, channels), F32),
@@ -415,6 +471,7 @@
             vmem((2, rows, channels), BF16),
             vmem((2, 4, 2 * middle, LANES), F32),
             vmem((4, 2 * middle, LANES), F32),
+            vmem((2, 2 * middle, 2 * LANES), BF16),
             vmem((2, 4, rows, channels), F32),
             vmem((2, rows, channels), BF16),
             vmem((2, 4, rows, channels), BF16),
@@ -424,16 +481,18 @@
             vmem((2, 2, rows // 2, channels), BF16),
             vmem((2, 2, rows // 2, channels), BF16),
             dma((7,)),
-            dma((2,)),
-            dma((2,)),
-            dma((3, 2, 3)),
-            dma((3, 2, 3)),
-            dma((2, 4)),
-            dma((2, 4)),
-            dma((2, 2, 2)),
-            dma((2, 2, 2)),
             dma((2, 2)),
             dma((2, 2)),
+            dma((2, 2, 3)),
+            dma((2, 2, 3)),
+            dma((3, 3)),
+            dma((3, 3)),
+            dma((3, 4)),
+            dma((3, 4)),
+            dma((3, 2, 2)),
+            dma((3, 2, 2)),
+            dma((3, 2)),
+            dma((3, 2)),
         ],
         compiler_params=pltpu.CompilerParams(
             collective_id=0, has_side_effects=True, vmem_limit_bytes=62 * 1024 * 1024

time: 39.8 us -> 38.4 us (0.965)
  local copies, waits for them, and re-layouts: 1.67 us -> 0.71 us
  Pallas kernels: 38 us -> 37.5 us
    unnamed x1, local copies, waits for them, and re-layouts: 1.67 us -> 0.71 us
    pallas_call x1, Pallas kernels: 38 us -> 37.5 us  [fused(): pl.pallas_call(kernel, out_shape=pltpu.VMEM((2, rows, channels), BF16), i...]
where the time goes in v3:
time: 38.4 us; the launch traced here: 38.2 us
  Pallas kernels  37.5 us (98%)
  local copies, waits for them, and re-layouts  0.71 us (2%)
    pallas_call x1, Pallas kernels, fused(): pl.pallas_call(kernel, out_shape=pltpu.VMEM((2, rows, channels), BF16), i...  37.5 us

profile of v3, /device:TPU:0, one launch (start us, length us, event | category | flops | bytes accessed | tf_op | source)
XLA Modules:
  0.0 38.2 jit_solution(3264462290783498274)
XLA Ops:
  0.0 37.5 %hyena.1 = bf16[2,128,512]{2,1,0:T(8,128)(2,1)S(1)} custom-call(bf16[2,3,128,512]{3,2,1,0:T(8,128)(2,1)} %bitcast.10, bf16[3,7,512]{2,1,0:T(8,128)(2,1)} %bitcast.12, bf16[2,128,512]{2,1,0:T(8,128)(2,1)} %bitcast.11, f32[1,512]{1,0:T(1,128)} %bitcast.13, bf16[512,4096]{1,0:T(8,128)(2,1)} %weight_hbm.1, bf16[2,512,256]{2,1,0:T(8,128)(2,1)} %constant.4.clone.forward_hbm, ...), custom_call_target="tpu_custom_call" | custom-call | tf_op jit(solution)/shard_map/hyena/pallas_call | solution.py:451
  37.5 0.7 %copy.10 = bf16[2,1,128,512]{3,2,1,0:T(8,128)(2,1)} copy(bf16[2,1,128,512]{3,2,1,0:T(8,128)(2,1)S(1)} %bitcast.9) | data formatting | bytes 524288

commit v4 on v3

--- a/solution.py
+++ b/solution.py
@@ -63,6 +63,7 @@
     filter_spec,
     key_spec,
     summed_spec,
+    early,
     own,
     act,
     pair_out,
@@ -116,8 +117,6 @@
 
     for load in loads[4:]:
         load.start()
-    for load in loads[:4]:
-        load.wait()
     pending = []
 
     def remote(src, dst, send, recv, device):
@@ -125,50 +124,9 @@
             src_ref=src, dst_ref=dst, send_sem=send, recv_sem=recv, device_id=device, device_id_type=MESH
         )
 
-    def widen(h):
-        for s in range(3):
-            wide[h, s, RIM:] = x_ref[h, s].astype(F32)
-
-    widen(0)
-    widen(1)
-    tail = slice(rows, rows + RIM)
-    rims = {}
-    for kind, streams in ((0, (1, 2)), (1, (0, 0))):
-        for h in range(2):
-            rim_out[kind, h] = jnp.concatenate([wide[h, s, tail] for s in streams], axis=0).astype(BF16)
-            rims[kind, h] = remote(
-                rim_out.at[kind, h],
-                halo.at[kind, h],
-                halo_send.at[kind, h],
-                halo_recv.at[kind, h],
-                ((z + (1 if h == 0 else 3)) % PAIRS, ch),
-            )
-
-    def send_rims(kind):
-        @pl.when(z < PAIRS - 1)
-        def _():
-            rims[kind, 0].start()
-
-        @pl.when(z > 0)
-        def _():
-            rims[kind, 1].start()
-
-    def take_rim(kind, h):
-        has = z > 0 if h == 0 else z < PAIRS - 1
-
-        @pl.when(has)
-        def _():
-            rims[kind, h].wait_recv()
-
-        @pl.when(jnp.logical_not(has))
-        def _():
-            halo[kind, h] = jnp.zeros(halo.shape[2:], BF16) if h == 0 else rim_out[kind, 0]
-
-        both = halo[kind, h].astype(F32)
-        for m, s in enumerate((1, 2) if kind == 0 else (0,)):
-            wide[h, s, :RIM] = both[m * RIM : (m + 1) * RIM]
-
-    send_rims(0)
+    def keep(kind, source, h):
+        mine_rows, mine_lanes = place(h, z)
+        moved[kind, h, mine_rows, mine_lanes] = source[h, :, lane_slice(z)]
 
     def place(h, owner, first_row=0, count=None):
         block = owner if h == 0 else PAIRS - 1 - owner
@@ -184,7 +142,7 @@
     def scatter(kind, source, h):
         mine_rows, mine_lanes = place(h, z)
         copies = []
-        for o in (2, 1, 3):
+        for o in (3, 2, 1):
             target = (z + o) % PAIRS
             copy = remote(
                 source.at[h, :, lane_slice(target)],
@@ -195,10 +153,59 @@
             )
             copy.start()
             copies.append(copy)
-        moved[kind, h, mine_rows, mine_lanes] = source[h, :, lane_slice(z)]
         pending.extend(copies)
         return copies
 
+    filter_copies, key_copies = [None, None], [None, None]
+    filter_copies[0] = scatter(0, filter_hbm, 0)
+    loads[0].wait()
+
+    def widen(h):
+        for s in range(3):
+            wide[h, s, RIM:] = x_ref[h, s].astype(F32)
+
+    tails = [[x_ref[h, s, rows - 2 * RIM :].astype(F32)[RIM:] for s in range(3)] for h in range(2)]
+    rims = {}
+    for kind, streams in ((0, (1, 2)), (1, (0, 0))):
+        for h in range(2):
+            rim_out[kind, h] = jnp.concatenate([tails[h][s] for s in streams], axis=0).astype(BF16)
+            rims[kind, h] = remote(
+                rim_out.at[kind, h],
+                halo.at[kind, h],
+                halo_send.at[kind, h],
+                halo_recv.at[kind, h],
+                ((z + (1 if h == 0 else 3)) % PAIRS, ch),
+            )
+
+    def send_rims(kind):
+        @pl.when(z < PAIRS - 1)
+        def _():
+            rims[kind, 0].start()
+
+        @pl.when(z > 0)
+        def _():
+            rims[kind, 1].start()
+
+    def take_rim(kind, h):
+        has = z > 0 if h == 0 else z < PAIRS - 1
+
+        @pl.when(has)
+        def _():
+            rims[kind, h].wait_recv()
+
+        @pl.when(jnp.logical_not(has))
+        def _():
+            halo[kind, h] = jnp.zeros(halo.shape[2:], BF16) if h == 0 else rim_out[kind, 0]
+
+        both = halo[kind, h].astype(F32)
+        for m, s in enumerate((1, 2) if kind == 0 else (0,)):
+            wide[h, s, :RIM] = both[m * RIM : (m + 1) * RIM]
+
+    send_rims(0)
+    widen(0)
+    widen(1)
+
+    loads[2].wait()
     tap_rows = [taps_ref[s].astype(F32) for s in range(3)]
 
     def taps_of(h, s, cols):
@@ -219,13 +226,15 @@
         for cols in columns:
             queries[h, :, cols] = taps_of(h, 0, cols)
 
-    filter_copies, key_copies = [None, None], [None, None]
-    filter_copies[0] = scatter(0, filter_ref, 0)
     take_rim(0, 0)
     make_keys(0)
     key_copies[0] = scatter(1, gated, 0)
+    keep(1, gated, 0)
     send_rims(1)
-    filter_copies[1] = scatter(0, filter_ref, 1)
+    filter_copies[1] = scatter(0, filter_hbm, 1)
+    loads[1].wait()
+    keep(0, filter_ref, 0)
+    keep(0, filter_ref, 1)
     take_rim(0, 1)
     make_keys(1)
     loads[4].wait()
@@ -256,21 +265,35 @@
         for m in range(2):
             key_spec[2 * h + m] = both[:, m * LANES : (m + 1) * LANES]
 
+    def pair_products(i, sources, re_rows, im_rows):
+        real, imag = None, None
+        for j in sources:
+            ra, ia = filter_spec[1, i - j, re_rows], filter_spec[1, i - j, im_rows]
+            rb, ib = key_spec[j, re_rows], key_spec[j, im_rows]
+            re, im = ra * rb - ia * ib, ra * ib + ia * rb
+            real = re if real is None else real + re
+            imag = im if imag is None else imag + im
+        return real, imag
+
+    strips = [
+        (slice(start, start + STRIP), slice(middle + start, middle + start + STRIP))
+        for start in range(0, middle, STRIP)
+    ]
+
+    def early_products():
+        for m in range(2):
+            for re_rows, im_rows in strips:
+                early[m, re_rows], early[m, im_rows] = pair_products(2 + m, (0, 1), re_rows, im_rows)
+
     def products(h):
         for m in range(2):
             i = 2 * h + m
             cols = slice(m * LANES, (m + 1) * LANES)
-            for start in range(0, middle, STRIP):
-                re_rows = slice(start, start + STRIP)
-                im_rows = slice(middle + start, middle + start + STRIP)
-                real, imag = None, None
-                for j in range(i + 1):
-                    ra, ia = filter_spec[1, i - j, re_rows], filter_spec[1, i - j, im_rows]
-                    rb, ib = key_spec[j, re_rows], key_spec[j, im_rows]
-                    re, im = ra * rb - ia * ib, ra * ib + ia * rb
-                    real = re if real is None else real + re
-                    imag = im if imag is None else imag + im
-                for where, value in ((re_rows, real), (im_rows, imag)):
+            for re_rows, im_rows in strips:
+                sums = pair_products(i, range(2 * h, i + 1), re_rows, im_rows)
+                for where, value in zip((re_rows, im_rows), sums):
+                    if h == 1:
+                        value = value + early[m, where]
                     high = value.astype(BF16)
                     summed_spec[0, where, cols] = high
                     summed_spec[1, where, cols] = (value - high.astype(F32)).astype(BF16)
@@ -307,6 +330,7 @@
     filter_spectra(0)
     key_spectra(0)
     key_copies[1] = scatter(1, gated, 1)
+    keep(1, gated, 1)
     loads[5].wait()
     convolve(0)
     send_back(0)
@@ -315,11 +339,13 @@
     take_rim(1, 1)
     make_queries(1)
     filter_spectra(1)
+    early_products()
     key_spectra(1)
     convolve(1)
     send_back(1)
     send_back(2)
     loads[6].wait()
+    loads[3].wait()
 
     steps = [(1, 1), (0, 1), (1, 0), (0, 0)]
     pair_copies = {}
@@ -358,8 +384,11 @@
             copy.start()
             pair_copies[q, t] = copy
             pending.append(copy)
-        for t, step in enumerate(steps):
-            own[h, t, span] = dot(rows_in, weights_for(step, core))
+
+    def project_own(q, t):
+        h, first_row, count = chunks[q]
+        span = slice(first_row, first_row + count)
+        own[h, t, span] = dot(act[h, span], weights_for(steps[t], core))
 
     first_copies, second_copies = {}, {}
 
@@ -371,6 +400,7 @@
         h, where = chunks[q][0], slot_rows(q)
         for t, way, slot in ((0, 0, 0), (0, 1, 0), (1, 0, 1), (2, 1, 1)):
             if (t, way) != (0, 1):
+                project_own(q, t)
                 pair_copies[q, t].wait_recv()
             first_out[h, way, slot, where] = pair_sum(q, t, way).astype(BF16)
             copy = remote(
@@ -383,6 +413,7 @@
             copy.start()
             first_copies[q, way, slot] = copy
             pending.append(copy)
+        project_own(q, 3)
 
     def second(q):
         h, where = chunks[q][0], slot_rows(q)
@@ -472,6 +503,7 @@
             vmem((2, 4, 2 * middle, LANES), F32),
             vmem((4, 2 * middle, LANES), F32),
             vmem((2, 2 * middle, 2 * LANES), BF16),
+            vmem((2, 2 * middle, LANES), F32),
             vmem((2, 4, rows, channels), F32),
             vmem((2, rows, channels), BF16),
             vmem((2, 4, rows, channels), BF16),

time: 38.4 us -> 40.7 us (1.060)
  Pallas kernels: 37.5 us -> 39.9 us
    pallas_call x1, Pallas kernels: 37.5 us -> 39.9 us  [fused(): pl.pallas_call(kernel, out_shape=pltpu.VMEM((2, rows, channels), BF16), i...]
where the time goes in v4:
time: 40.7 us; the launch traced here: 40.6 us
  Pallas kernels  39.9 us (98%)
  local copies, waits for them, and re-layouts  0.71 us (2%)
    pallas_call x1, Pallas kernels, fused(): pl.pallas_call(kernel, out_shape=pltpu.VMEM((2, rows, channels), BF16), i...  39.9 us

profile of v4, /device:TPU:0, one launch (start us, length us, event | category | flops | bytes accessed | tf_op | source)
XLA Modules:
  0.0 40.6 jit_solution(4878618622109285389)
XLA Ops:
  0.0 39.9 %hyena.1 = bf16[2,128,512]{2,1,0:T(8,128)(2,1)S(1)} custom-call(bf16[2,3,128,512]{3,2,1,0:T(8,128)(2,1)} %bitcast.10, bf16[3,7,512]{2,1,0:T(8,128)(2,1)} %bitcast.12, bf16[2,128,512]{2,1,0:T(8,128)(2,1)} %bitcast.11, f32[1,512]{1,0:T(1,128)} %bitcast.13, bf16[512,4096]{1,0:T(8,128)(2,1)} %weight_hbm.1, bf16[2,512,256]{2,1,0:T(8,128)(2,1)} %constant.4.clone.forward_hbm, ...), custom_call_target="tpu_custom_call" | custom-call | tf_op jit(solution)/shard_map/hyena/pallas_call | solution.py:482
  39.9 0.7 %copy.10 = bf16[2,1,128,512]{3,2,1,0:T(8,128)(2,1)} copy(bf16[2,1,128,512]{3,2,1,0:T(8,128)(2,1)S(1)} %bitcast.9) | data formatting | bytes 524288

commit v5 on v4

--- a/solution.py
+++ b/solution.py
@@ -142,7 +142,7 @@
     def scatter(kind, source, h):
         mine_rows, mine_lanes = place(h, z)
         copies = []
-        for o in (3, 2, 1):
+        for o in (2, 1, 3):
             target = (z + o) % PAIRS
             copy = remote(
                 source.at[h, :, lane_slice(target)],
@@ -157,7 +157,6 @@
         return copies
 
     filter_copies, key_copies = [None, None], [None, None]
-    filter_copies[0] = scatter(0, filter_hbm, 0)
     loads[0].wait()
 
     def widen(h):
@@ -202,6 +201,8 @@
             wide[h, s, :RIM] = both[m * RIM : (m + 1) * RIM]
 
     send_rims(0)
+    loads[1].wait()
+    filter_copies[0] = scatter(0, filter_ref, 0)
     widen(0)
     widen(1)
 
@@ -231,8 +232,7 @@
     key_copies[0] = scatter(1, gated, 0)
     keep(1, gated, 0)
     send_rims(1)
-    filter_copies[1] = scatter(0, filter_hbm, 1)
-    loads[1].wait()
+    filter_copies[1] = scatter(0, filter_ref, 1)
     keep(0, filter_ref, 0)
     keep(0, filter_ref, 1)
     take_rim(0, 1)

time: 40.7 us -> 38.1 us (0.936)
  Pallas kernels: 39.9 us -> 37.2 us
    pallas_call x1, Pallas kernels: 39.9 us -> 37.2 us  [fused(): pl.pallas_call(kernel, out_shape=pltpu.VMEM((2, rows, channels), BF16), i...]
where the time goes in v5:
time: 38.1 us; the launch traced here: 37.9 us
  Pallas kernels  37.2 us (98%)
  local copies, waits for them, and re-layouts  0.71 us (2%)
    pallas_call x1, Pallas kernels, fused(): pl.pallas_call(kernel, out_shape=pltpu.VMEM((2, rows, channels), BF16), i...  37.2 us

profile of v5, /device:TPU:0, one launch (start us, length us, event | category | flops | bytes accessed | tf_op | source)
XLA Modules:
  0.0 37.9 jit_solution(2658055772553986192)
XLA Ops:
  0.0 37.2 %hyena.1 = bf16[2,128,512]{2,1,0:T(8,128)(2,1)S(1)} custom-call(bf16[2,3,128,512]{3,2,1,0:T(8,128)(2,1)} %bitcast.10, bf16[3,7,512]{2,1,0:T(8,128)(2,1)} %bitcast.12, bf16[2,128,512]{2,1,0:T(8,128)(2,1)} %bitcast.11, f32[1,512]{1,0:T(1,128)} %bitcast.13, bf16[512,4096]{1,0:T(8,128)(2,1)} %weight_hbm.1, bf16[2,512,256]{2,1,0:T(8,128)(2,1)} %constant.4.clone.forward_hbm, ...), custom_call_target="tpu_custom_call" | custom-call | tf_op jit(solution)/shard_map/hyena/pallas_call | solution.py:482
  37.2 0.7 %copy.10 = bf16[2,1,128,512]{3,2,1,0:T(8,128)(2,1)} copy(bf16[2,1,128,512]{3,2,1,0:T(8,128)(2,1)S(1)} %bitcast.9) | data formatting | bytes 524288

commit v6 on v5

--- a/solution.py
+++ b/solution.py
@@ -73,6 +73,7 @@
     second_out,
     second_in,
     local_sem,
+    filter_sem,
     halo_send,
     halo_recv,
     move_send,
@@ -86,7 +87,8 @@
     second_send,
     second_recv,
 ):
-    rows, channels = gated.shape[1:]
+    rows = gated.shape[2]
+    channels = weight.shape[0]
     taps = taps_ref.shape[1]
     middle = forward.shape[2]
     z = lax.axis_index("ctx")
@@ -100,13 +102,20 @@
     beside_x = (z, ch_of(y, 1 - x, core))
     beside_y = (z, ch_of(1 - y, x, core))
 
-    sources = (x_hbm, filter_hbm, taps_hbm, skip_hbm, forward_hbm, inverse_hbm, weight_hbm)
-    places = (x_ref, filter_ref, taps_ref, skip_ref, forward, inverse, weight)
+    sources = (x_hbm, taps_hbm, skip_hbm, forward_hbm, inverse_hbm, weight_hbm)
+    places = (x_ref, taps_ref, skip_ref, forward, inverse, weight)
     loads = [
         pltpu.make_async_copy(source, target, local_sem.at[i])
         for i, (source, target) in enumerate(zip(sources, places))
     ]
-    for load in loads[:4]:
+    filter_loads = [
+        pltpu.make_async_copy(
+            filter_hbm.at[h, :, pl.ds(c * LANES, LANES)], filter_ref.at[h, c], filter_sem.at[h, c]
+        )
+        for h in range(2)
+        for c in range(channels // LANES)
+    ]
+    for load in (loads[0], *filter_loads, loads[1], loads[2]):
         load.start()
 
     barrier = pltpu.get_barrier_semaphore()
@@ -115,7 +124,7 @@
         pl.semaphore_signal(barrier, inc=1, device_id=peer, device_id_type=MESH)
     pl.semaphore_wait(barrier, len(peers))
 
-    for load in loads[4:]:
+    for load in loads[3:]:
         load.start()
     pending = []
 
@@ -125,28 +134,18 @@
         )
 
     def keep(kind, source, h):
-        mine_rows, mine_lanes = place(h, z)
-        moved[kind, h, mine_rows, mine_lanes] = source[h, :, lane_slice(z)]
-
-    def place(h, owner, first_row=0, count=None):
-        block = owner if h == 0 else PAIRS - 1 - owner
-        count = rows if count is None else count
-        return (
-            pl.ds(pl.multiple_of(block % 2 * rows + first_row, count), count),
-            pl.ds(pl.multiple_of(block // 2 * LANES, LANES), LANES),
-        )
-
-    def lane_slice(owner):
-        return pl.ds(pl.multiple_of(owner * LANES, LANES), LANES)
+        moved[kind, h, block_of(h, z)] = source[h, z]
+
+    def block_of(h, owner):
+        return owner if h == 0 else PAIRS - 1 - owner
 
     def scatter(kind, source, h):
-        mine_rows, mine_lanes = place(h, z)
         copies = []
         for o in (2, 1, 3):
             target = (z + o) % PAIRS
             copy = remote(
-                source.at[h, :, lane_slice(target)],
-                moved.at[kind, h, mine_rows, mine_lanes],
+                source.at[h, target],
+                moved.at[kind, h, block_of(h, z)],
                 move_send.at[kind, h, o - 1],
                 move_recv.at[kind, h, o - 1],
                 (target, ch),
@@ -201,12 +200,13 @@
             wide[h, s, :RIM] = both[m * RIM : (m + 1) * RIM]
 
     send_rims(0)
-    loads[1].wait()
+    for load in filter_loads:
+        load.wait()
     filter_copies[0] = scatter(0, filter_ref, 0)
     widen(0)
     widen(1)
 
-    loads[2].wait()
+    loads[1].wait()
     tap_rows = [taps_ref[s].astype(F32) for s in range(3)]
 
     def taps_of(h, s, cols):
@@ -220,8 +220,8 @@
     columns = [slice(a, a + LANES) for a in range(0, channels, LANES)]
 
     def make_keys(h):
-        for cols in columns:
-            gated[h, :, cols] = (taps_of(h, 1, cols) * taps_of(h, 2, cols)).astype(BF16)
+        for c, cols in enumerate(columns):
+            gated[h, c] = (taps_of(h, 1, cols) * taps_of(h, 2, cols)).astype(BF16)
 
     def make_queries(h):
         for cols in columns:
@@ -237,12 +237,14 @@
     keep(0, filter_ref, 1)
     take_rim(0, 1)
     make_keys(1)
-    loads[4].wait()
+    loads[3].wait()
 
     signs = (1 - 2 * (lax.broadcasted_iota(jnp.int32, (middle, LANES), 0) % 2)).astype(F32)
 
     def spectrum(kind, h):
-        data = moved[kind, h]
+        data = jnp.concatenate(
+            [jnp.concatenate([moved[kind, h, 2 * m], moved[kind, h, 2 * m + 1]], axis=0) for m in range(2)], axis=1
+        )
         return dot(forward[0], data) + dot(forward[1], data)
 
     def filter_spectra(h):
@@ -306,18 +308,16 @@
         copies = []
         for o in (2, 1, 3):
             target = (z + o) % PAIRS
-            its_rows, its_lanes = place(h, target, first_row, count)
             copy = remote(
-                convolved.at[h, its_rows, its_lanes],
-                back.at[h, pl.ds(first_row, count), lane_slice(z)],
+                convolved.at[h, block_of(h, target), pl.ds(first_row, count)],
+                back.at[h, z, pl.ds(first_row, count)],
                 back_send.at[q, o - 1],
                 back_recv.at[q, o - 1],
                 (target, ch),
             )
             copy.start()
             copies.append(copy)
-        mine_rows, mine_lanes = place(h, z, first_row, count)
-        back[h, pl.ds(first_row, count), lane_slice(z)] = convolved[h, mine_rows, mine_lanes]
+        back[h, z, pl.ds(first_row, count)] = convolved[h, block_of(h, z), pl.ds(first_row, count)]
         pending.extend(copies)
         back_copies[q] = copies
 
@@ -325,15 +325,18 @@
         products(h)
         high, low = summed_spec[0], summed_spec[1]
         result = dot(inverse[0], high) + dot(inverse[0], low) + dot(inverse[1], high)
-        convolved[h] = result.astype(BF16)
+        result = result.astype(BF16)
+        for block in range(PAIRS):
+            m, part = divmod(block, 2)
+            convolved[h, block] = result[part * rows : (part + 1) * rows, m * LANES : (m + 1) * LANES]
 
     filter_spectra(0)
     key_spectra(0)
+    loads[4].wait()
+    convolve(0)
+    send_back(0)
     key_copies[1] = scatter(1, gated, 1)
     keep(1, gated, 1)
-    loads[5].wait()
-    convolve(0)
-    send_back(0)
     take_rim(1, 0)
     make_queries(0)
     take_rim(1, 1)
@@ -344,8 +347,8 @@
     convolve(1)
     send_back(1)
     send_back(2)
-    loads[6].wait()
-    loads[3].wait()
+    loads[5].wait()
+    loads[2].wait()
 
     steps = [(1, 1), (0, 1), (1, 0), (0, 0)]
     pair_copies = {}
@@ -368,8 +371,8 @@
         span = slice(first_row, first_row + count)
         for copy in back_copies[q]:
             copy.wait_recv()
-        for cols in columns:
-            summed = back[h, span, cols].astype(F32) + skip_ref[:, cols] * gated[h, span, cols].astype(F32)
+        for c, cols in enumerate(columns):
+            summed = back[h, c, span].astype(F32) + skip_ref[:, cols] * gated[h, c, span].astype(F32)
             act[h, span, cols] = (queries[h, span, cols] * summed).astype(BF16)
         rows_in = act[h, span]
         for t, step in enumerate(steps):
@@ -475,6 +478,7 @@
     streams = jnp.transpose(features[:, 0], (0, 2, 1, 3))
     taps = jnp.transpose(short_weight, (1, 0, 2))
     forward, inverse = odd_tables(middle)
+    blocked = (2, channels // LANES, rows, LANES)
     in_vmem = pl.BlockSpec(memory_space=pltpu.VMEM)
     in_hbm = pl.BlockSpec(memory_space=pl.ANY)
     vmem = pltpu.VMEM
@@ -487,7 +491,7 @@
         scratch_shapes=[
             vmem(streams.shape, BF16),
             vmem(taps.shape, BF16),
-            vmem((2, rows, channels), BF16),
+            vmem(blocked, BF16),
             vmem((1, channels), F32),
             vmem(out_weight.shape, BF16),
             vmem(forward.shape, BF16),
@@ -495,11 +499,11 @@
             vmem((2, 2, 2 * RIM, channels), BF16),
             vmem((2, 2, 2 * RIM, channels), BF16),
             vmem((2, 3, RIM + rows, channels), F32),
-            vmem((2, rows, channels), BF16),
+            vmem(blocked, BF16),
             vmem((2, rows, channels), F32),
-            vmem((2, 2, middle, 2 * LANES), BF16),
-            vmem((2, middle, 2 * LANES), BF16),
-            vmem((2, rows, channels), BF16),
+            vmem((2, *blocked), BF16),
+            vmem(blocked, BF16),
+            vmem(blocked, BF16),
             vmem((2, 4, 2 * middle, LANES), F32),
             vmem((4, 2 * middle, LANES), F32),
             vmem((2, 2 * middle, 2 * LANES), BF16),
@@ -512,7 +516,8 @@
             vmem((2, 2, 2, rows // 2, channels), BF16),
             vmem((2, 2, rows // 2, channels), BF16),
             vmem((2, 2, rows // 2, channels), BF16),
-            dma((7,)),
+            dma((6,)),
+            dma((2, channels // LANES)),
             dma((2, 2)),
             dma((2, 2)),
             dma((2, 2, 3)),

time: 38.1 us -> 39.3 us (1.031)
  Pallas kernels: 37.2 us -> 38.4 us
    pallas_call x1, Pallas kernels: 37.2 us -> 38.4 us  [fused(): pl.pallas_call(kernel, out_shape=pltpu.VMEM((2, rows, channels), BF16), i...]
where the time goes in v6:
time: 39.3 us; the launch traced here: 39.1 us
  Pallas kernels  38.4 us (98%)
  local copies, waits for them, and re-layouts  0.71 us (2%)
    pallas_call x1, Pallas kernels, fused(): pl.pallas_call(kernel, out_shape=pltpu.VMEM((2, rows, channels), BF16), i...  38.4 us

profile of v6, /device:TPU:0, one launch (start us, length us, event | category | flops | bytes accessed | tf_op | source)
XLA Modules:
  0.0 39.1 jit_solution(4474566296873635495)
XLA Ops:
  0.0 38.4 %hyena.1 = bf16[2,128,512]{2,1,0:T(8,128)(2,1)S(1)} custom-call(bf16[2,3,128,512]{3,2,1,0:T(8,128)(2,1)} %bitcast.10, bf16[3,7,512]{2,1,0:T(8,128)(2,1)} %bitcast.12, bf16[2,128,512]{2,1,0:T(8,128)(2,1)} %bitcast.11, f32[1,512]{1,0:T(1,128)} %bitcast.13, bf16[512,4096]{1,0:T(8,128)(2,1)} %weight_hbm.1, bf16[2,512,256]{2,1,0:T(8,128)(2,1)} %constant.4.clone.forward_hbm, ...), custom_call_target="tpu_custom_call" | custom-call | tf_op jit(solution)/shard_map/hyena/pallas_call | solution.py:486
  38.4 0.7 %copy.10 = bf16[2,1,128,512]{3,2,1,0:T(8,128)(2,1)} copy(bf16[2,1,128,512]{3,2,1,0:T(8,128)(2,1)S(1)} %bitcast.9) | data formatting | bytes 524288

commit v7 on v6

--- a/solution.py
+++ b/solution.py
@@ -237,6 +237,8 @@
     keep(0, filter_ref, 1)
     take_rim(0, 1)
     make_keys(1)
+    key_copies[1] = scatter(1, gated, 1)
+    keep(1, gated, 1)
     loads[3].wait()
 
     signs = (1 - 2 * (lax.broadcasted_iota(jnp.int32, (middle, LANES), 0) % 2)).astype(F32)
@@ -335,8 +337,6 @@
     loads[4].wait()
     convolve(0)
     send_back(0)
-    key_copies[1] = scatter(1, gated, 1)
-    keep(1, gated, 1)
     take_rim(1, 0)
     make_queries(0)
     take_rim(1, 1)

time: 39.3 us -> 38.1 us (0.969)
  Pallas kernels: 38.4 us -> 37.3 us
    pallas_call x1, Pallas kernels: 38.4 us -> 37.3 us  [fused(): pl.pallas_call(kernel, out_shape=pltpu.VMEM((2, rows, channels), BF16), i...]
where the time goes in v7:
time: 38.1 us; the launch traced here: 38 us
  Pallas kernels  37.3 us (98%)
  local copies, waits for them, and re-layouts  0.71 us (2%)
    pallas_call x1, Pallas kernels, fused(): pl.pallas_call(kernel, out_shape=pltpu.VMEM((2, rows, channels), BF16), i...  37.3 us

profile of v7, /device:TPU:0, one launch (start us, length us, event | category | flops | bytes accessed | tf_op | source)
XLA Modules:
  0.0 38.0 jit_solution(11040267333429666616)
XLA Ops:
  0.0 37.3 %hyena.1 = bf16[2,128,512]{2,1,0:T(8,128)(2,1)S(1)} custom-call(bf16[2,3,128,512]{3,2,1,0:T(8,128)(2,1)} %bitcast.10, bf16[3,7,512]{2,1,0:T(8,128)(2,1)} %bitcast.12, bf16[2,128,512]{2,1,0:T(8,128)(2,1)} %bitcast.11, f32[1,512]{1,0:T(1,128)} %bitcast.13, bf16[512,4096]{1,0:T(8,128)(2,1)} %weight_hbm.1, bf16[2,512,256]{2,1,0:T(8,128)(2,1)} %constant.4.clone.forward_hbm, ...), custom_call_target="tpu_custom_call" | custom-call | tf_op jit(solution)/shard_map/hyena/pallas_call | solution.py:486
  37.3 0.7 %copy.10 = bf16[2,1,128,512]{3,2,1,0:T(8,128)(2,1)} copy(bf16[2,1,128,512]{3,2,1,0:T(8,128)(2,1)S(1)} %bitcast.9) | data formatting | bytes 524288

commit v8 on v7

--- a/solution.py
+++ b/solution.py
@@ -302,7 +302,7 @@
                     summed_spec[0, where, cols] = high
                     summed_spec[1, where, cols] = (value - high.astype(F32)).astype(BF16)
 
-    chunks = [(0, 0, rows), (1, 0, rows // 2), (1, rows // 2, rows // 2)]
+    chunks = [(h, first_row, rows // 2) for h in range(2) for first_row in (0, rows // 2)]
     back_copies = {}
 
     def send_back(q):
@@ -337,6 +337,7 @@
     loads[4].wait()
     convolve(0)
     send_back(0)
+    send_back(1)
     take_rim(1, 0)
     make_queries(0)
     take_rim(1, 1)
@@ -345,8 +346,8 @@
     early_products()
     key_spectra(1)
     convolve(1)
-    send_back(1)
     send_back(2)
+    send_back(3)
     loads[5].wait()
     loads[2].wait()
 
@@ -452,11 +453,15 @@
     project(2)
     second(0)
     first(2)
+    project(3)
     second(1)
+    first(3)
     finish(0)
     second(2)
     finish(1)
+    second(3)
     finish(2)
+    finish(3)
 
     @pl.when(z < PAIRS - 1)
     def _():
@@ -522,14 +527,14 @@
             dma((2, 2)),
             dma((2, 2, 3)),
             dma((2, 2, 3)),
-            dma((3, 3)),
-            dma((3, 3)),
-            dma((3, 4)),
-            dma((3, 4)),
-            dma((3, 2, 2)),
-            dma((3, 2, 2)),
-            dma((3, 2)),
-            dma((3, 2)),
+            dma((4, 3)),
+            dma((4, 3)),
+            dma((4, 4)),
+            dma((4, 4)),
+            dma((4, 2, 2)),
+            dma((4, 2, 2)),
+            dma((4, 2)),
+            dma((4, 2)),
         ],
         compiler_params=pltpu.CompilerParams(
             collective_id=0, has_side_effects=True, vmem_limit_bytes=62 * 1024 * 1024

time: 38.1 us -> 37.8 us (level)
  Pallas kernels: 37.3 us -> 36.9 us
where the time goes in v8:
time: 37.8 us; the launch traced here: 37.6 us
  Pallas kernels  36.9 us (98%)
  local copies, waits for them, and re-layouts  0.71 us (2%)
    pallas_call x1, Pallas kernels, fused(): pl.pallas_call(kernel, out_shape=pltpu.VMEM((2, rows, channels), BF16), i...  36.9 us

profile of v8, /device:TPU:0, one launch (start us, length us, event | category | flops | bytes accessed | tf_op | source)
XLA Modules:
  0.0 37.6 jit_solution(6512196732018132001)
XLA Ops:
  0.0 36.9 %hyena.1 = bf16[2,128,512]{2,1,0:T(8,128)(2,1)S(1)} custom-call(bf16[2,3,128,512]{3,2,1,0:T(8,128)(2,1)} %bitcast.10, bf16[3,7,512]{2,1,0:T(8,128)(2,1)} %bitcast.12, bf16[2,128,512]{2,1,0:T(8,128)(2,1)} %bitcast.11, f32[1,512]{1,0:T(1,128)} %bitcast.13, bf16[512,4096]{1,0:T(8,128)(2,1)} %weight_hbm.1, bf16[2,512,256]{2,1,0:T(8,128)(2,1)} %constant.4.clone.forward_hbm, ...), custom_call_target="tpu_custom_call" | custom-call | tf_op jit(solution)/shard_map/hyena/pallas_call | solution.py:491
  36.9 0.7 %copy.10 = bf16[2,1,128,512]{3,2,1,0:T(8,128)(2,1)} copy(bf16[2,1,128,512]{3,2,1,0:T(8,128)(2,1)S(1)} %bitcast.9) | data formatting | bytes 524288

commit v9 on v8

--- a/solution.py
+++ b/solution.py
@@ -139,9 +139,9 @@
     def block_of(h, owner):
         return owner if h == 0 else PAIRS - 1 - owner
 
-    def scatter(kind, source, h):
+    def scatter(kind, source, h, offsets=(2, 1, 3)):
         copies = []
-        for o in (2, 1, 3):
+        for o in offsets:
             target = (z + o) % PAIRS
             copy = remote(
                 source.at[h, target],
@@ -237,7 +237,7 @@
     keep(0, filter_ref, 1)
     take_rim(0, 1)
     make_keys(1)
-    key_copies[1] = scatter(1, gated, 1)
+    key_copies[1] = scatter(1, gated, 1, (2,))
     keep(1, gated, 1)
     loads[3].wait()
 
@@ -338,6 +338,7 @@
     convolve(0)
     send_back(0)
     send_back(1)
+    key_copies[1] += scatter(1, gated, 1, (1, 3))
     take_rim(1, 0)
     make_queries(0)
     take_rim(1, 1)

time: 37.8 us -> 39.1 us (1.034)
  Pallas kernels: 36.9 us -> 38.3 us
    pallas_call x1, Pallas kernels: 36.9 us -> 38.3 us  [fused(): pl.pallas_call(kernel, out_shape=pltpu.VMEM((2, rows, channels), BF16), i...]
where the time goes in v9:
time: 39.1 us; the launch traced here: 39 us
  Pallas kernels  38.3 us (98%)
  local copies, waits for them, and re-layouts  0.71 us (2%)
    pallas_call x1, Pallas kernels, fused(): pl.pallas_call(kernel, out_shape=pltpu.VMEM((2, rows, channels), BF16), i...  38.3 us

profile of v9, /device:TPU:0, one launch (start us, length us, event | category | flops | bytes accessed | tf_op | source)
XLA Modules:
  0.0 39.0 jit_solution(15135763734091637600)
XLA Ops:
  0.0 38.3 %hyena.1 = bf16[2,128,512]{2,1,0:T(8,128)(2,1)S(1)} custom-call(bf16[2,3,128,512]{3,2,1,0:T(8,128)(2,1)} %bitcast.10, bf16[3,7,512]{2,1,0:T(8,128)(2,1)} %bitcast.12, bf16[2,128,512]{2,1,0:T(8,128)(2,1)} %bitcast.11, f32[1,512]{1,0:T(1,128)} %bitcast.13, bf16[512,4096]{1,0:T(8,128)(2,1)} %weight_hbm.1, bf16[2,512,256]{2,1,0:T(8,128)(2,1)} %constant.4.clone.forward_hbm, ...), custom_call_target="tpu_custom_call" | custom-call | tf_op jit(solution)/shard_map/hyena/pallas_call | solution.py:492
  38.3 0.7 %copy.10 = bf16[2,1,128,512]{3,2,1,0:T(8,128)(2,1)} copy(bf16[2,1,128,512]{3,2,1,0:T(8,128)(2,1)S(1)} %bitcast.9) | data formatting | bytes 524288

commit v10 on v8

--- a/solution.py
+++ b/solution.py
@@ -203,6 +203,7 @@
     for load in filter_loads:
         load.wait()
     filter_copies[0] = scatter(0, filter_ref, 0)
+    send_rims(1)
     widen(0)
     widen(1)
 
@@ -231,7 +232,6 @@
     make_keys(0)
     key_copies[0] = scatter(1, gated, 0)
     keep(1, gated, 0)
-    send_rims(1)
     filter_copies[1] = scatter(0, filter_ref, 1)
     keep(0, filter_ref, 0)
     keep(0, filter_ref, 1)
@@ -239,6 +239,9 @@
     make_keys(1)
     key_copies[1] = scatter(1, gated, 1)
     keep(1, gated, 1)
+    for h in range(2):
+        take_rim(1, h)
+        make_queries(h)
     loads[3].wait()
 
     signs = (1 - 2 * (lax.broadcasted_iota(jnp.int32, (middle, LANES), 0) % 2)).astype(F32)
@@ -338,10 +341,6 @@
     convolve(0)
     send_back(0)
     send_back(1)
-    take_rim(1, 0)
-    make_queries(0)
-    take_rim(1, 1)
-    make_queries(1)
     filter_spectra(1)
     early_products()
     key_spectra(1)

time: 37.8 us -> 37.5 us (level)
  no operation moved by 1% of the time
where the time goes in v10:
time: 37.5 us; the launch traced here: 37.4 us
  Pallas kernels  36.6 us (98%)
  local copies, waits for them, and re-layouts  0.71 us (2%)
    pallas_call x1, Pallas kernels, fused(): pl.pallas_call(kernel, out_shape=pltpu.VMEM((2, rows, channels), BF16), i...  36.6 us

profile of v10, /device:TPU:0, one launch (start us, length us, event | category | flops | bytes accessed | tf_op | source)
XLA Modules:
  0.0 37.4 jit_solution(3124157938703886353)
XLA Ops:
  0.0 36.6 %hyena.1 = bf16[2,128,512]{2,1,0:T(8,128)(2,1)S(1)} custom-call(bf16[2,3,128,512]{3,2,1,0:T(8,128)(2,1)} %bitcast.10, bf16[3,7,512]{2,1,0:T(8,128)(2,1)} %bitcast.12, bf16[2,128,512]{2,1,0:T(8,128)(2,1)} %bitcast.11, f32[1,512]{1,0:T(1,128)} %bitcast.13, bf16[512,4096]{1,0:T(8,128)(2,1)} %weight_hbm.1, bf16[2,512,256]{2,1,0:T(8,128)(2,1)} %constant.4.clone.forward_hbm, ...), custom_call_target="tpu_custom_call" | custom-call | tf_op jit(solution)/shard_map/hyena/pallas_call | solution.py:490
  36.7 0.7 %copy.10 = bf16[2,1,128,512]{3,2,1,0:T(8,128)(2,1)} copy(bf16[2,1,128,512]{3,2,1,0:T(8,128)(2,1)S(1)} %bitcast.9) | data formatting | bytes 524288
